TPU v7x, 32 devices: a whole 2x2x4 slice. The times are simulated.
32 devices in a mesh: sec: 8 (over y, x, core), tile: 4 (over z).
Axes of the slice: x: 2, y: 2, z: 4, core: 2. Of those that a mesh axis runs over, the one named last changes fastest.
Arguments:
- image: bfloat16 [8, 4096, 1024], P('sec', 'tile'), as said below
- fwd_offset: int32 [8, 2, 32, 8], P('sec', None, 'tile'), may hold values from -16 to 16
- bwd_offset: int32 [8, 2, 32, 8], P('sec', None, 'tile'), may hold values from -16 to 16
- valid: int32 [8, 32, 8], P('sec', 'tile'), may hold values 0 or 1
Outputs:
- pair_flow: float32 [8, 2, 32, 8], P('sec', None, 'tile')
- mesh_shift: float32 [8, 2, 32, 8], P('sec', None, 'tile')
Inputs may be any that keep to these rules, and one draw needn't show every extreme that they name: `image`: pixel intensities of order one.
All inputs are finite; a program needn't handle non-finite values. No bound on the sum of `valid` on one device may be relied on, other than what follows from the above.
Results may differ from a plain program's by a relative error of at most 0.0003.
Values may be sent and summed in bfloat16 or wider, within the bound.
No kernel may reach another device: no remote copies, remote signals or barrier semaphores. Data moves between devices by JAX's collectives and lax.ppermute only.
A program may use at most 128 MiB of HBM per device.

v0:
```python
import math

import jax
import jax.numpy as jnp
from jax import lax
from jax.sharding import PartitionSpec as P

PATCH = 128
OFFMAX = 16
ITERS = 3


highest_peak = lax.Precision.HIGHEST


def with_halo(block, sides, width):
    for axis, dim in sides:
        count = lax.axis_size(axis)
        forward = [(i, i + 1) for i in range(count - 1)]
        backward = [(target, source) for source, target in forward]
        low = lax.ppermute(
            lax.slice_in_dim(block, block.shape[dim] - width, None, axis=dim), axis, forward
        )
        high = lax.ppermute(lax.slice_in_dim(block, 0, width, axis=dim), axis, backward)
        block = jnp.concatenate([low, block, high], axis=dim)
    return block


def shifted(array, axis, by):
    length = lax.axis_size(axis)
    pairs = [(i, i + by) for i in range(length) if 0 <= i + by < length]
    return lax.ppermute(array, axis, pairs)


def entering(array, axis, combine, identity):
    length, place = (lax.axis_size(axis), lax.axis_index(axis))
    everything = lax.all_gather(array, axis)
    start = jnp.broadcast_to(jnp.asarray(identity, array.dtype), array.shape)

    def hop(k, before):
        reached = k < place
        new = combine(before, everything[k])
        return jnp.where(reached, new, before)

    return lax.fori_loop(0, length, hop, start)


def tables(size):
    index = jnp.arange(size, dtype=jnp.int32)
    product = index[:, None] * index[None, :] % size
    angle = product.astype(jnp.float32) * (2.0 * math.pi / size)
    return (jnp.cos(angle), jnp.sin(angle))


def spectrum(flow_field, cosine_table, sine_table):
    left_cosine = jnp.einsum("hp,spz->shz", cosine_table, flow_field, precision=highest_peak)
    left_sine = jnp.einsum("hp,spz->shz", sine_table, flow_field, precision=highest_peak)
    real_part = jnp.einsum(
        "nuk,kv->nuv", left_cosine, cosine_table, precision=highest_peak
    ) - jnp.einsum("nuk,kv->nuv", left_sine, sine_table, precision=highest_peak)
    imag_part = -(
        jnp.einsum("nuk,kv->nuv", left_cosine, sine_table, precision=highest_peak)
        + jnp.einsum("nuk,kv->nuv", left_sine, cosine_table, precision=highest_peak)
    )
    return (real_part, imag_part)


def centroids(first, second):
    size = first.shape[-1]
    cosine_table, sine_table = tables(size)
    left = first.astype(jnp.float32)
    left = left - jnp.mean(left, axis=(1, 2), keepdims=True)
    right = second.astype(jnp.float32)
    right = right - jnp.mean(right, axis=(1, 2), keepdims=True)
    left_re, left_im = spectrum(left, cosine_table, sine_table)
    right_re, right_im = spectrum(right, cosine_table, sine_table)
    cross_real = left_re * right_re + left_im * right_im
    cross_imaginary = left_re * right_im - left_im * right_re
    outer_cosine = jnp.einsum(
        "hp,spz->shz", cosine_table, cross_real, precision=highest_peak
    ) - jnp.einsum("hp,spz->shz", sine_table, cross_imaginary, precision=highest_peak)
    outer_sine = jnp.einsum(
        "hp,spz->shz", sine_table, cross_real, precision=highest_peak
    ) + jnp.einsum("hp,spz->shz", cosine_table, cross_imaginary, precision=highest_peak)
    corr = (
        jnp.einsum("nuk,kv->nuv", outer_cosine, cosine_table, precision=highest_peak)
        - jnp.einsum("nuk,kv->nuv", outer_sine, sine_table, precision=highest_peak)
    ) / (size * size)
    power = corr * corr
    total = jnp.sum(power, axis=(1, 2)) + size * size * 1e-06
    index = jnp.arange(size)
    lags = ((index + size // 2) % size - size // 2).astype(jnp.float32)
    row_c = jnp.sum(power * lags[None, :, None], axis=(1, 2)) / total
    col_c = jnp.sum(power * lags[None, None, :], axis=(1, 2)) / total
    return jnp.stack([row_c, col_c], axis=1)


def regions(padded_field, pr_dev, col_count):
    sec_dev = padded_field.shape[0]
    extra_rows = (pr_dev + 1) * PATCH - padded_field.shape[1]
    extra_cols = (col_count + 1) * PATCH - padded_field.shape[2]
    padded_field = jnp.pad(padded_field, ((0, 0), (0, extra_rows), (0, extra_cols)))
    width = padded_field.shape[2]
    span = PATCH + 2 * OFFMAX
    main_rows = padded_field[:, 0 : pr_dev * PATCH].reshape(sec_dev, pr_dev, PATCH, width)
    tail_rows = padded_field[:, PATCH : pr_dev * PATCH + PATCH].reshape(
        sec_dev, pr_dev, PATCH, width
    )[:, :, 0 : 2 * OFFMAX]
    strips = jnp.concatenate([main_rows, tail_rows], axis=2)
    main_cols = strips[..., 0 : col_count * PATCH].reshape(sec_dev, pr_dev, span, col_count, PATCH)
    tail_cols = strips[..., PATCH : col_count * PATCH + PATCH].reshape(
        sec_dev, pr_dev, span, col_count, PATCH
    )[..., 0 : 2 * OFFMAX]
    blocks = jnp.concatenate([main_cols, tail_cols], axis=4)
    return blocks.transpose(0, 1, 3, 2, 4).reshape(sec_dev * pr_dev * col_count, span, span)


def centered(block_set):
    return block_set[:, OFFMAX : OFFMAX + PATCH, OFFMAX : OFFMAX + PATCH]


def selected(block_set, row_off, col_off):
    span = block_set.shape[1]
    target = jnp.arange(span, dtype=jnp.int32)[None, None, :]
    base = jnp.arange(PATCH, dtype=jnp.int32)[None, :, None] + OFFMAX
    pick_rows = (target == base + row_off[:, None, None]).astype(jnp.bfloat16)
    pick_cols = (target == base + col_off[:, None, None]).astype(jnp.bfloat16)
    row_cut = jnp.einsum(
        "nyu,nuv->nyv", pick_rows, block_set, preferred_element_type=jnp.float32
    ).astype(jnp.bfloat16)
    return jnp.einsum(
        "nyv,nxv->nyx", row_cut, pick_cols, preferred_element_type=jnp.float32
    ).astype(jnp.bfloat16)


def body(image, fwd_offset, bwd_offset, valid):
    sec_dev = image.shape[0]
    pr_dev = valid.shape[1]
    col_count = valid.shape[2]
    own = with_halo(image, (("tile", 1),), OFFMAX)
    arriving = shifted(own, "sec", -1)
    after = jnp.concatenate([own[1:], arriving], axis=0)
    own = jnp.pad(own, ((0, 0), (0, 0), (OFFMAX, OFFMAX)))
    after = jnp.pad(after, ((0, 0), (0, 0), (OFFMAX, OFFMAX)))
    own_blocks = regions(own, pr_dev, col_count)
    after_blocks = regions(after, pr_dev, col_count)
    fy = fwd_offset[:, 0].ravel()
    fx = fwd_offset[:, 1].ravel()
    by = bwd_offset[:, 0].ravel()
    bx = bwd_offset[:, 1].ravel()
    forward = centroids(centered(own_blocks), selected(after_blocks, fy, fx))
    forward = forward + jnp.stack([fy, fx], axis=1).astype(jnp.float32)
    backward = centroids(centered(after_blocks), selected(own_blocks, by, bx))
    backward = backward + jnp.stack([by, bx], axis=1).astype(jnp.float32)
    flows = (
        (0.5 * (forward - backward)).T.reshape(2, sec_dev, pr_dev, col_count).transpose(1, 0, 2, 3)
    )
    global_sec = lax.axis_index("sec") * sec_dev + jnp.arange(sec_dev, dtype=jnp.int32)
    notlast = (global_sec < sec_dev * lax.axis_size("sec") - 1).astype(jnp.float32)
    pair_flow = flows * notlast[:, None, None, None]
    weight = valid.astype(jnp.float32) * notlast[:, None, None]
    sums, counts = lax.psum(
        (jnp.sum(weight[:, None] * pair_flow, axis=(2, 3)), jnp.sum(weight, axis=(1, 2))), "tile"
    )
    mean_flow = sums / jnp.maximum(counts, 1.0)[:, None]
    local_before = jnp.cumsum(mean_flow, axis=0) - mean_flow
    group_total = jnp.sum(mean_flow, axis=0)
    carried = entering(
        group_total, "sec", lambda earlier, later: earlier + later, jnp.zeros((2,), jnp.float32)
    )
    start = carried[None, :] + local_before
    shift = jnp.broadcast_to(start[:, :, None, None], pair_flow.shape).astype(jnp.float32)
    weight4 = weight[:, None]
    global_row = lax.axis_index("tile") * pr_dev + jnp.arange(pr_dev, dtype=jnp.int32)
    has_up = (global_row > 0).astype(jnp.float32)[None, None, :, None]
    has_down = (global_row < pr_dev * lax.axis_size("tile") - 1).astype(jnp.float32)[
        None, None, :, None
    ]
    for step in range(ITERS):
        spring = weight4 * (shift + pair_flow)
        stacked = jnp.concatenate([shift, spring, weight4], axis=1)
        border = with_halo(stacked, (("sec", 0), ("tile", 2)), 1)
        above = border[1:-1, 0:2, :-2, :]
        below = border[1:-1, 0:2, 2:, :]
        plane = has_up * (above - shift) + has_down * (below - shift)
        cols = shift[:, :, :, 1:] - shift[:, :, :, :-1]
        plane = (
            plane
            + jnp.pad(-cols, ((0, 0), (0, 0), (0, 0), (1, 0)))
            + jnp.pad(cols, ((0, 0), (0, 0), (0, 0), (0, 1)))
        )
        next_shift = border[2:, 0:2, 1:-1, :]
        prev_spring = border[:-2, 2:4, 1:-1, :]
        prev_weight = border[:-2, 4:5, 1:-1, :]
        between = weight4 * (next_shift - shift - pair_flow) - (prev_weight * shift - prev_spring)
        shift = shift + 0.25 * (plane + between)
    return (pair_flow, shift)


def solution(mesh):
    return jax.shard_map(
        body,
        mesh=mesh,
        in_specs=(
            P("sec", "tile", None),
            P("sec", None, "tile", None),
            P("sec", None, "tile", None),
            P("sec", "tile", None),
        ),
        out_specs=(P("sec", None, "tile", None), P("sec", None, "tile", None)),
        check_vma=False,
    )
```

profile of v0, /device:TPU:0, one launch (start us, length us, event | category | flops | bytes accessed | tf_op | source)
XLA Modules:
  0.0 420.4 jit_solution(8652309361907436927)
XLA Ops:
  50.3 8.9 %fusion.44 = f32[64,128,128]{2,1,0:T(8,128)} fusion(f32[64,128,128]{2,1,0:T(8,128)S(1)} %fusion.4), kind=kOutput, calls=%fused_computation.60 | convolution fusion | flops 1610842112 | bytes 8388608 | tf_op jit(solution)/shard_map/nuk,kv->nuv/dot_general | solution.py:63
  59.2 8.6 %fusion.46 = f32[64,128,128]{2,1,0:T(8,128)} fusion(f32[64,128,128]{2,1,0:T(8,128)S(1)} %fusion.4), kind=kOutput, calls=%fused_computation.62 | convolution fusion | flops 1610842112 | bytes 8388608 | tf_op jit(solution)/shard_map/nuk,kv->nuv/dot_general | solution.py:60
  75.5 7.2 %fusion.10 = f32[64,128,128]{2,1,0:T(8,128)S(1)} fusion(bf16[64,128,128]{2,1,0:T(8,128)(2,1)S(1)} %get-tuple-element.175, f32[64]{0:T(128)S(1)} %broadcast_multiply_fusion), kind=kOutput, calls=%fused_computation.26 | convolution fusion | flops 1612939264 | bytes 6291712 | tf_op jit(solution)/shard_map/hp,spz->shz/dot_general | solution.py:57
  82.6 7.2 %fusion.16 = f32[64,128,128]{2,1,0:T(8,128)S(1)} fusion(f32[64,128,128]{2,1,0:T(8,128)S(1)} %fusion.10), kind=kOutput, calls=%fused_computation.32 | convolution fusion | flops 1610842112 | bytes 8388608 | tf_op jit(solution)/shard_map/nuk,kv->nuv/dot_general | solution.py:63
  89.9 7.9 %fusion.11 = f32[64,128,128]{2,1,0:T(8,128)S(1)} fusion(bf16[64,128,128]{2,1,0:T(8,128)(2,1)S(1)} %get-tuple-element.175, f32[64]{0:T(128)S(1)} %broadcast_multiply_fusion), kind=kOutput, calls=%fused_computation.27 | convolution fusion | flops 1612939264 | bytes 6291712 | tf_op jit(solution)/shard_map/hp,spz->shz/dot_general | solution.py:56
  97.8 8.7 %fusion.18 = f32[64,128,128]{2,1,0:T(8,128)} fusion(f32[64,128,128]{2,1,0:T(8,128)S(1)} %fusion.10), kind=kOutput, calls=%fused_computation.34 | convolution fusion | flops 1610842112 | bytes 8388608 | tf_op jit(solution)/shard_map/nuk,kv->nuv/dot_general | solution.py:60
  106.5 8.8 %fusion.67 = f32[64,128,128]{2,1,0:T(8,128)} fusion(f32[64,128,128]{2,1,0:T(8,128)S(1)} %copy-done.10, f32[64,128,128]{2,1,0:T(8,128)S(1)} %copy-done.2), kind=kOutput, calls=%fused_computation.101 | convolution fusion | flops 1611890688 | bytes 12582912 | tf_op jit(solution)/shard_map/nuk,kv->nuv/dot_general | solution.py:62
  115.4 8.8 %fusion.64 = f32[64,128,128]{2,1,0:T(8,128)} fusion(f32[64,128,128]{2,1,0:T(8,128)S(1)} %copy-done.9, f32[64,128,128]{2,1,0:T(8,128)S(1)} %copy-done.2), kind=kOutput, calls=%fused_computation.100 | convolution fusion | flops 1611890688 | bytes 12582912 | tf_op jit(solution)/shard_map/nuk,kv->nuv/dot_general | solution.py:58
  124.2 8.7 %fusion.85 = f32[64,128,128]{2,1,0:T(8,128)} fusion(f32[64,128,128]{2,1,0:T(8,128)S(1)} %fusion.16, f32[64,128,128]{2,1,0:T(8,128)S(1)} %fusion.11), kind=kOutput, calls=%fused_computation.107 | convolution fusion | flops 1611890688 | bytes 12582912 | tf_op jit(solution)/shard_map/nuk,kv->nuv/dot_general | solution.py:62
  164.2 7.2 %fusion.6 = f32[64,128,128]{2,1,0:T(8,128)S(1)} fusion(bf16[64,128,128]{2,1,0:T(8,128)(2,1)S(1)} %get-tuple-element.177, f32[64]{0:T(128)S(1)} %broadcast_multiply_fusion.2), kind=kOutput, calls=%fused_computation.22 | convolution fusion | flops 1612939264 | bytes 6291712 | tf_op jit(solution)/shard_map/hp,spz->shz/dot_general | solution.py:57
  171.4 7.3 %fusion.7 = f32[64,128,128]{2,1,0:T(8,128)S(1)} fusion(bf16[64,128,128]{2,1,0:T(8,128)(2,1)S(1)} %get-tuple-element.177, f32[64]{0:T(128)S(1)} %broadcast_multiply_fusion.2), kind=kOutput, calls=%fused_computation.23 | convolution fusion | flops 1612939264 | bytes 6291712 | tf_op jit(solution)/shard_map/hp,spz->shz/dot_general | solution.py:56
  178.7 7.2 %fusion.36 = f32[64,128,128]{2,1,0:T(8,128)S(1)} fusion(f32[64,128,128]{2,1,0:T(8,128)S(1)} %fusion.6), kind=kOutput, calls=%fused_computation.52 | convolution fusion | flops 1610842112 | bytes 8388608 | tf_op jit(solution)/shard_map/nuk,kv->nuv/dot_general | solution.py:63
  185.9 8.8 %fusion.38 = f32[64,128,128]{2,1,0:T(8,128)} fusion(f32[64,128,128]{2,1,0:T(8,128)S(1)} %fusion.6), kind=kOutput, calls=%fused_computation.54 | convolution fusion | flops 1610842112 | bytes 8388608 | tf_op jit(solution)/shard_map/nuk,kv->nuv/dot_general | solution.py:60
  201.5 9.2 %multiply_subtract_fusion.1 = (f32[64,128,128]{2,1,0:T(8,128)S(1)}, f32[64,128,128]{2,1,0:T(8,128)S(1)}) fusion(f32[64,128,128]{2,1,0:T(8,128)S(1)} %copy-done.5, f32[64,128,128]{2,1,0:T(8,128)S(1)} %copy-done.6, f32[64,128,128]{2,1,0:T(8,128)S(1)} %fusion.73, f32[64,128,128]{2,1,0:T(8,128)} %fusion.38, f32[64,128,128]{2,1,0:T(8,128)S(1)} %fusion.7), kind=kOutput, calls=%fused_computation.80 | convolution fusion | flops 1620279296 | bytes 29360128 | tf_op jit(solution)/shard_map/nuk,kv->nuv/dot_general | solution.py:58
  210.7 8.9 %fusion.125 = f32[64,128,128]{2,1,0:T(8,128)} fusion(f32[64,128,128]{2,1,0:T(8,128)S(1)} %get-tuple-element.143), kind=kOutput, calls=%fused_computation.143 | convolution fusion | flops 1610842112 | bytes 8388608 | tf_op jit(solution)/shard_map/hp,spz->shz/dot_general | solution.py:82
  219.7 8.5 %fusion.149 = f32[64,128,128]{2,1,0:T(8,128)} fusion(f32[64,128,128]{2,1,0:T(8,128)S(1)} %get-tuple-element.143), kind=kOutput, calls=%fused_computation.167 | convolution fusion | flops 1610842112 | bytes 8388608 | tf_op jit(solution)/shard_map/hp,spz->shz/dot_general | solution.py:79
  228.2 8.4 %fusion.146 = f32[64,128,128]{2,1,0:T(8,128)} fusion(f32[64,128,128]{2,1,0:T(8,128)S(1)} %get-tuple-element.142), kind=kOutput, calls=%fused_computation.164 | convolution fusion | flops 1610842112 | bytes 8388608 | tf_op jit(solution)/shard_map/hp,spz->shz/dot_general | solution.py:84
  236.6 8.7 %fusion.127 = f32[64,128,128]{2,1,0:T(8,128)} fusion(f32[64,128,128]{2,1,0:T(8,128)S(1)} %get-tuple-element.142), kind=kOutput, calls=%fused_computation.145 | convolution fusion | flops 1610842112 | bytes 8388608 | tf_op jit(solution)/shard_map/hp,spz->shz/dot_general | solution.py:81
  255.3 7.1 %fusion.24 = f32[64,128,128]{2,1,0:T(8,128)S(1)} fusion(f32[64,128,128]{2,1,0:T(8,128)S(1)} %fusion.8), kind=kOutput, calls=%fused_computation.40 | convolution fusion | flops 1610842112 | bytes 8388608 | tf_op jit(solution)/shard_map/nuk,kv->nuv/dot_general | solution.py:63
  262.4 6.9 %fusion.26 = f32[64,128,128]{2,1,0:T(8,128)S(1)} fusion(f32[64,128,128]{2,1,0:T(8,128)S(1)} %fusion.8), kind=kOutput, calls=%fused_computation.42 | convolution fusion | flops 1610842112 | bytes 8388608 | tf_op jit(solution)/shard_map/nuk,kv->nuv/dot_general | solution.py:60
  269.2 7.5 %fusion.79 = f32[64,128,128]{2,1,0:T(8,128)S(1)} fusion(f32[64,128,128]{2,1,0:T(8,128)S(1)} %fusion.24, f32[64,128,128]{2,1,0:T(8,128)S(1)} %fusion.9), kind=kOutput, calls=%fused_computation.105 | convolution fusion | flops 1611890688 | bytes 12582912 | tf_op jit(solution)/shard_map/nuk,kv->nuv/dot_general | solution.py:62
  276.8 7.2 %fusion.76 = f32[64,128,128]{2,1,0:T(8,128)S(1)} fusion(f32[64,128,128]{2,1,0:T(8,128)S(1)} %fusion.26, f32[64,128,128]{2,1,0:T(8,128)S(1)} %fusion.9), kind=kOutput, calls=%fused_computation.104 | convolution fusion | flops 1611890688 | bytes 12582912 | tf_op jit(solution)/shard_map/nuk,kv->nuv/dot_general | solution.py:58
  284.0 9.2 %multiply_subtract_fusion = (f32[64,128,128]{2,1,0:T(8,128)S(1)}, f32[64,128,128]{2,1,0:T(8,128)S(1)}) fusion(f32[64,128,128]{2,1,0:T(8,128)S(1)} %fusion.79, f32[64,128,128]{2,1,0:T(8,128)S(1)} %fusion.76, f32[64,128,128]{2,1,0:T(8,128)S(1)} %copy-done.4, f32[64,128,128]{2,1,0:T(8,128)} %fusion.18, f32[64,128,128]{2,1,0:T(8,128)S(1)} %copy-done.1), kind=kOutput, calls=%fused_computation.73 | convolution fusion | flops 1620279296 | bytes 29360128 | tf_op jit(solution)/shard_map/nuk,kv->nuv/dot_general | solution.py:58
  293.3 7.0 %fusion.114 = f32[64,128,128]{2,1,0:T(8,128)S(1)} fusion(f32[64,128,128]{2,1,0:T(8,128)S(1)} %get-tuple-element.145), kind=kOutput, calls=%fused_computation.132 | convolution fusion | flops 1610842112 | bytes 8388608 | tf_op jit(solution)/shard_map/hp,spz->shz/dot_general | solution.py:82
  300.3 7.4 %fusion.138 = f32[64,128,128]{2,1,0:T(8,128)S(1)} fusion(f32[64,128,128]{2,1,0:T(8,128)S(1)} %get-tuple-element.145), kind=kOutput, calls=%fused_computation.156 | convolution fusion | flops 1610842112 | bytes 8388608 | tf_op jit(solution)/shard_map/hp,spz->shz/dot_general | solution.py:79
  314.5 7.0 %fusion.116 = f32[64,128,128]{2,1,0:T(8,128)S(1)} fusion(f32[64,128,128]{2,1,0:T(8,128)S(1)} %get-tuple-element.144), kind=kOutput, calls=%fused_computation.134 | convolution fusion | flops 1610842112 | bytes 8388608 | tf_op jit(solution)/shard_map/hp,spz->shz/dot_general | solution.py:81
  321.5 6.9 %fusion.32 = f32[64,128,128]{2,1,0:T(8,128)S(1)} fusion(f32[64,128,128]{2,1,0:T(8,128)S(1)} %copy-done.7, f32[64,128,128]{2,1,0:T(8,128)S(1)} %copy-done.8), kind=kOutput, calls=%fused_computation.48 | convolution fusion | flops 1611890688 | bytes 12582912 | tf_op jit(solution)/shard_map/nuk,kv->nuv/dot_general | solution.py:87
  328.4 7.3 %fusion.12 = f32[64,128,128]{2,1,0:T(8,128)S(1)} fusion(f32[64,128,128]{2,1,0:T(8,128)S(1)} %fusion.114, f32[64,128,128]{2,1,0:T(8,128)S(1)} %fusion.135), kind=kOutput, calls=%fused_computation.28 | convolution fusion | flops 1611890688 | bytes 12582912 | tf_op jit(solution)/shard_map/nuk,kv->nuv/dot_general | solution.py:87
  335.8 7.5 %multiply_multiply_fusion.1 = f32[64,128,128]{2,1,0:T(8,128)S(1)} fusion(f32[64,128,128]{2,1,0:T(8,128)S(1)} %fusion.32, f32[64,128,128]{2,1,0:T(8,128)S(1)} %copy-done.11, f32[64,128,128]{2,1,0:T(8,128)S(1)} %copy-done.12), kind=kOutput, calls=%fused_computation.77 | convolution fusion | flops 1615036416 | bytes 16777216 | tf_op jit(solution)/shard_map/nuk,kv->nuv/dot_general | solution.py:86
  343.3 9.0 %multiply_reduce_fusion.1 = (f32[64]{0:T(128)S(1)}, f32[64]{0:T(128)S(1)}, f32[64]{0:T(128)S(1)}, f32[64]{0:T(128)S(1)}, f32[64]{0:T(128)S(1)}, /*index=5*/f32[64]{0:T(128)S(1)}) fusion(f32[128]{0:T(128)S(1)} %fusion.264, f32[64,128,128]{2,1,0:T(8,128)S(1)} %multiply_multiply_fusion.1, f32[64,128,128]{2,1,0:T(8,128)S(1)} %fusion.12, ...), kind=kOutput, calls=%fused_computation.69 | convolution fusion | flops 1625521792 | bytes 16779264 | tf_op jit(solution)/shard_map/nuk,kv->nuv/dot_general | solution.py:86
  352.4 13.7 %all-reduce.10 = (f32[1,2]{1,0:T(1,128)S(1)}, f32[1]{0:T(128)}) all-reduce(f32[1,2]{1,0:T(1,128)S(1)} %bitcast.266, f32[1]{0:T(128)} %bitcast.34), channel_id=1, replica_groups=mesh['sec'=8,'tile'=4] {'tile'}, use_global_device_ids=true, to_apply=%region_11.12 | all-reduce | flops 3 | bytes 24 | tf_op jit(solution)/shard_map/psum | solution.py:162
  366.8 9.7 %all-gather = f32[8,1,2]{2,1,0:T(1,128)S(1)} all-gather(f32[1,1,2]{2,1,0:T(1,128)S(1)} %fusion.434), channel_id=1, replica_groups=mesh['sec'=8,'tile'=4] {'sec'}, dimensions={0}, use_global_device_ids=true | all-gather | bytes 72 | tf_op jit(solution)/shard_map/all_gather | solution.py:37
  (148 shorter events, 155.7 us)
Async XLA Ops:
  1.4 9.8 %collective-permute-start = (bf16[1,16,1024]{2,1,0:T(8,128)(2,1)S(1)}, bf16[1,16,1024]{2,1,0:T(8,128)(2,1)S(1)}, u32[]{:S(2)}, u32[]{:S(2)}) collective-permute-start(bf16[1,16,1024]{2,1,0:T(8,128)(2,1)S(1)} %get-tuple-element.155), channel_id=1, source_target_pairs={{0,1},{1,2},{2,3},{4,5},{5,6},{6,7},{8,9},{9,10},{10,11},{12,13},{... | collective-permute-start | bytes 98312 | tf_op jit(solution)/shard_map/ppermute | solution.py:21
  6.3 8.7 %collective-permute-start.1 = (bf16[1,16,1024]{2,1,0:T(8,128)(2,1)S(1)}, bf16[1,16,1024]{2,1,0:T(8,128)(2,1)S(1)}, u32[]{:S(2)}, u32[]{:S(2)}) collective-permute-start(bf16[1,16,1024]{2,1,0:T(8,128)(2,1)S(1)} %get-tuple-element.154), channel_id=1, source_target_pairs={{1,0},{2,1},{3,2},{5,4},{6,5},{7,6},{9,8},{10,9},{11,10},{13,12},{... | collective-permute-start | bytes 98312 | tf_op jit(solution)/shard_map/ppermute | solution.py:24
  38.8 5.7 %copy-start.3 = (bf16[1,8,160,8,160]{2,4,3,1,0:T(8,128)(2,1)}, bf16[1,8,160,8,160]{2,4,3,1,0:T(8,128)(2,1)S(1)}, u32[]{:S(2)}) copy-start(bf16[1,8,160,8,160]{2,4,3,1,0:T(8,128)(2,1)S(1)} %pad_maximum_fusion) | copy-start | bytes 9830404
  67.9 65.0 %collective-permute-start.2 = (bf16[1,1056,1024]{2,1,0:T(8,128)(2,1)}, bf16[1,1056,1024]{2,1,0:T(8,128)(2,1)}, u32[]{:S(2)}, u32[]{:S(2)}) collective-permute-start(bf16[1,1056,1024]{2,1,0:T(8,128)(2,1)} %constant_dynamic-update-slice_fusion), channel_id=1, source_target_pairs={{4,0},{8,4},{12,8},{16,12},{20,16},{24,20},{28,24},{5,1},{9,5},{13... | collective-permute-start | bytes 6488072 | tf_op jit(solution)/shard_map/ppermute | solution.py:32
  97.8 26.4 %copy-start = (f32[64,128,128]{2,1,0:T(8,128)}, f32[64,128,128]{2,1,0:T(8,128)S(1)}, u32[]{:S(2)}) copy-start(f32[64,128,128]{2,1,0:T(8,128)S(1)} %fusion.11) | copy-start | bytes 12582916
  97.8 8.8 %copy-start.2 = (f32[64,128,128]{2,1,0:T(8,128)S(1)}, f32[64,128,128]{2,1,0:T(8,128)}, u32[]{:S(2)}) copy-start(f32[64,128,128]{2,1,0:T(8,128)} %fusion.5) | copy-start | bytes 12582916
  97.8 8.8 %copy-start.10 = (f32[64,128,128]{2,1,0:T(8,128)S(1)}, f32[64,128,128]{2,1,0:T(8,128)}, u32[]{:S(2)}) copy-start(f32[64,128,128]{2,1,0:T(8,128)} %fusion.44) | copy-start | bytes 12582916
  106.5 8.8 %copy-start.9 = (f32[64,128,128]{2,1,0:T(8,128)S(1)}, f32[64,128,128]{2,1,0:T(8,128)}, u32[]{:S(2)}) copy-start(f32[64,128,128]{2,1,0:T(8,128)} %fusion.46) | copy-start | bytes 12582916
  194.7 6.8 %copy-start.5 = (f32[64,128,128]{2,1,0:T(8,128)S(1)}, f32[64,128,128]{2,1,0:T(8,128)}, u32[]{:S(2)}) copy-start(f32[64,128,128]{2,1,0:T(8,128)} %fusion.67) | copy-start | bytes 12582916
  194.7 6.8 %copy-start.6 = (f32[64,128,128]{2,1,0:T(8,128)S(1)}, f32[64,128,128]{2,1,0:T(8,128)}, u32[]{:S(2)}) copy-start(f32[64,128,128]{2,1,0:T(8,128)} %fusion.64) | copy-start | bytes 12582916
  228.2 17.2 %slice-start = ((s8[5242880]{0:T(1024)(128)(4,1)}), s8[4194304]{0:T(1024)(128)(4,1)S(1)}, s32[]{:S(2)}) async-start(s8[5242880]{0:T(1024)(128)(4,1)} %bitcast.234), calls=%async_computation | async-start | bytes 8388608
  236.6 8.7 %slice-start.1 = ((s8[5242880]{0:T(1024)(128)(4,1)}), s8[1048576]{0:T(1024)(128)(4,1)S(1)}, s32[]{:S(2)}) async-start(s8[5242880]{0:T(1024)(128)(4,1)} %bitcast.234), calls=%async_computation.1 | async-start | bytes 2097152
  276.7 7.3 %copy-start.1 = (f32[64,128,128]{2,1,0:T(8,128)S(1)}, f32[64,128,128]{2,1,0:T(8,128)}, u32[]{:S(2)}) copy-start(f32[64,128,128]{2,1,0:T(8,128)} %copy-done) | copy-start | bytes 12582916
  276.8 7.3 %copy-start.4 = (f32[64,128,128]{2,1,0:T(8,128)S(1)}, f32[64,128,128]{2,1,0:T(8,128)}, u32[]{:S(2)}) copy-start(f32[64,128,128]{2,1,0:T(8,128)} %fusion.85) | copy-start | bytes 12582916
  314.5 7.0 %copy-start.7 = (f32[64,128,128]{2,1,0:T(8,128)S(1)}, f32[64,128,128]{2,1,0:T(8,128)}, u32[]{:S(2)}) copy-start(f32[64,128,128]{2,1,0:T(8,128)} %fusion.125) | copy-start | bytes 12582916
  314.5 7.0 %copy-start.8 = (f32[64,128,128]{2,1,0:T(8,128)S(1)}, f32[64,128,128]{2,1,0:T(8,128)}, u32[]{:S(2)}) copy-start(f32[64,128,128]{2,1,0:T(8,128)} %fusion.146) | copy-start | bytes 12582916
  328.4 7.4 %copy-start.11 = (f32[64,128,128]{2,1,0:T(8,128)S(1)}, f32[64,128,128]{2,1,0:T(8,128)}, u32[]{:S(2)}) copy-start(f32[64,128,128]{2,1,0:T(8,128)} %fusion.149) | copy-start | bytes 12582916
  328.4 7.4 %copy-start.12 = (f32[64,128,128]{2,1,0:T(8,128)S(1)}, f32[64,128,128]{2,1,0:T(8,128)}, u32[]{:S(2)}) copy-start(f32[64,128,128]{2,1,0:T(8,128)} %fusion.127) | copy-start | bytes 12582916
  366.8 53.3 %copy-start.13 = (f32[1,2,8,8]{3,2,1,0:T(8,128)}, f32[1,2,8,8]{3,2,1,0:T(8,128)S(1)}, u32[]{:S(2)}) copy-start(f32[1,2,8,8]{3,2,1,0:T(8,128)S(1)} %mul.583) | copy-start | bytes 1540
  377.0 3.6 collective-permute-start.3
  379.2 3.5 collective-permute-start.4
  382.8 5.9 %collective-permute-start.6 = (f32[3,5,1,8]{3,2,1,0:T(1,128)S(1)}, f32[3,5,1,8]{3,2,1,0:T(1,128)S(1)}, u32[]{:S(2)}, u32[]{:S(2)}) collective-permute-start(f32[3,5,1,8]{3,2,1,0:T(1,128)S(1)} %get-tuple-element.161), channel_id=1, source_target_pairs={{1,0},{2,1},{3,2},{5,4},{6,5},{7,6},{9,8},{10,9},{11,10},{13,12},{... | collective-permute-start | bytes 1448 | tf_op jit(solution)/shard_map/ppermute | solution.py:24
  384.1 5.9 %collective-permute-start.5 = (f32[3,5,1,8]{3,2,1,0:T(1,128)S(1)}, f32[3,5,1,8]{3,2,1,0:T(1,128)S(1)}, u32[]{:S(2)}, u32[]{:S(2)}) collective-permute-start(f32[3,5,1,8]{3,2,1,0:T(1,128)S(1)} %get-tuple-element.160), channel_id=1, source_target_pairs={{0,1},{1,2},{2,3},{4,5},{5,6},{6,7},{8,9},{9,10},{10,11},{12,13},{... | collective-permute-start | bytes 1448 | tf_op jit(solution)/shard_map/ppermute | solution.py:21
  390.2 4.7 %collective-permute-start.7 = (f32[1,5,8,8]{3,2,1,0:T(8,128)S(1)}, f32[1,5,8,8]{3,2,1,0:T(8,128)S(1)}, u32[]{:S(2)}, u32[]{:S(2)}) collective-permute-start(f32[1,5,8,8]{3,2,1,0:T(8,128)S(1)} %pad_maximum_fusion.8), channel_id=1, source_target_pairs={{0,4},{4,8},{8,12},{12,16},{16,20},{20,24},{24,28},{1,5},{5,9},{9,... | collective-permute-start | bytes 3848 | tf_op jit(solution)/shard_map/ppermute | solution.py:21
  393.5 3.7 collective-permute-start.8
  397.3 6.1 %collective-permute-start.10 = (f32[3,5,1,8]{3,2,1,0:T(1,128)S(1)}, f32[3,5,1,8]{3,2,1,0:T(1,128)S(1)}, u32[]{:S(2)}, u32[]{:S(2)}) collective-permute-start(f32[3,5,1,8]{3,2,1,0:T(1,128)S(1)} %get-tuple-element.159), channel_id=1, source_target_pairs={{1,0},{2,1},{3,2},{5,4},{6,5},{7,6},{9,8},{10,9},{11,10},{13,12},{... | collective-permute-start | bytes 1448 | tf_op jit(solution)/shard_map/ppermute | solution.py:24
  398.6 6.2 %collective-permute-start.9 = (f32[3,5,1,8]{3,2,1,0:T(1,128)S(1)}, f32[3,5,1,8]{3,2,1,0:T(1,128)S(1)}, u32[]{:S(2)}, u32[]{:S(2)}) collective-permute-start(f32[3,5,1,8]{3,2,1,0:T(1,128)S(1)} %get-tuple-element.158), channel_id=1, source_target_pairs={{0,1},{1,2},{2,3},{4,5},{5,6},{6,7},{8,9},{9,10},{10,11},{12,13},{... | collective-permute-start | bytes 1448 | tf_op jit(solution)/shard_map/ppermute | solution.py:21
  404.9 5.0 %collective-permute-start.11 = (f32[1,5,8,8]{3,2,1,0:T(8,128)S(1)}, f32[1,5,8,8]{3,2,1,0:T(8,128)S(1)}, u32[]{:S(2)}, u32[]{:S(2)}) collective-permute-start(f32[1,5,8,8]{3,2,1,0:T(8,128)S(1)} %pad_maximum_fusion.7), channel_id=1, source_target_pairs={{0,4},{4,8},{8,12},{12,16},{16,20},{20,24},{24,28},{1,5},{5,9},{9,... | collective-permute-start | bytes 3848 | tf_op jit(solution)/shard_map/ppermute | solution.py:21
  408.5 3.5 collective-permute-start.12
  411.9 6.1 %collective-permute-start.14 = (f32[3,5,1,8]{3,2,1,0:T(1,128)S(1)}, f32[3,5,1,8]{3,2,1,0:T(1,128)S(1)}, u32[]{:S(2)}, u32[]{:S(2)}) collective-permute-start(f32[3,5,1,8]{3,2,1,0:T(1,128)S(1)} %get-tuple-element.157), channel_id=1, source_target_pairs={{1,0},{2,1},{3,2},{5,4},{6,5},{7,6},{9,8},{10,9},{11,10},{13,12},{... | collective-permute-start | bytes 1448 | tf_op jit(solution)/shard_map/ppermute | solution.py:24
  413.2 6.2 %collective-permute-start.13 = (f32[3,5,1,8]{3,2,1,0:T(1,128)S(1)}, f32[3,5,1,8]{3,2,1,0:T(1,128)S(1)}, u32[]{:S(2)}, u32[]{:S(2)}) collective-permute-start(f32[3,5,1,8]{3,2,1,0:T(1,128)S(1)} %get-tuple-element.156), channel_id=1, source_target_pairs={{0,1},{1,2},{2,3},{4,5},{5,6},{6,7},{8,9},{9,10},{10,11},{12,13},{... | collective-permute-start | bytes 1448 | tf_op jit(solution)/shard_map/ppermute | solution.py:21
where the time goes:
time: 428 us; the launch traced here: 420 us
  matrix products  283 us (66%)
  local copies, waits for them, and re-layouts  42.2 us (10%)
  starting transfers between devices  38.9 us (9%)
  blocking collectives  23.3 us (5%)
  other arithmetic  20 us (5%)
  waiting for transfers between devices  10.6 us (2%)
    dot_general x4, matrix products, spectrum(): jnp.einsum('nuk,kv->nuv', left_cosine, cosine_table, precision=highest_peak)  34.5 us
    dot_general x4, matrix products, spectrum(): jnp.einsum('nuk,kv->nuv', left_sine, sine_table, precision=highest_peak)  33 us
    dot_general x4, matrix products, spectrum(): jnp.einsum('nuk,kv->nuv', left_cosine, sine_table, precision=highest_peak)  31.9 us
    dot_general x4, matrix products, spectrum(): jnp.einsum('nuk,kv->nuv', left_sine, cosine_table, precision=highest_peak)  30.4 us
    ppermute x7, starting transfers between devices, with_halo(): lax.ppermute(lax.slice_in_dim(block, block.shape[dim] - width, None, axis...  28.2 us
    dot_general x4, matrix products, spectrum(): jnp.einsum('hp,spz->shz', cosine_table, flow_field, precision=highest_peak)  25.2 us
    dot_general x4, matrix products, spectrum(): jnp.einsum('hp,spz->shz', sine_table, flow_field, precision=highest_peak)  22.7 us
    dot_general x2, matrix products, centroids(): jnp.einsum('nuk,kv->nuv', outer_cosine, cosine_table, precision=highest_p...  16.5 us
  transfers between devices with their start and end apart: 15, of which 6 were waited for; matrix products, arithmetic and copies ran while one was open for 17% of the time, Pallas kernels for 0%

commit v1 on v0

v1 whole, which is shorter than its diff:
```python
import functools

import jax
import jax.numpy as jnp
import ml_dtypes
import numpy as np
from jax import lax
from jax.experimental import pallas as pl
from jax.experimental.pallas import tpu as pltpu
from jax.sharding import PartitionSpec as P

PATCH = 128
HALF = PATCH // 2
OFFMAX = 16
ITERS = 3
LANES = 128
BF = jnp.bfloat16
F32 = jnp.float32


def split_table(table):
    high = table.astype(np.float32).astype(ml_dtypes.bfloat16)
    low = (table - high.astype(np.float64)).astype(np.float32).astype(ml_dtypes.bfloat16)
    return high, low


@functools.cache
def tables():
    place = np.arange(PATCH)
    quarter = np.sin(np.arange(PATCH // 4 + 1) * (2 * np.pi / PATCH))
    sine = np.concatenate([quarter, quarter[-2::-1], -quarter[1:], -quarter[-2:0:-1]])
    cosine = np.roll(sine, -PATCH // 4)
    basis = np.zeros((PATCH, PATCH))
    basis[0] = place % 2 == 0
    basis[HALF] = place % 2 == 1
    for u in range(1, HALF):
        basis[u] = cosine[(u * place) % PATCH]
        basis[HALF + u] = sine[(u * place) % PATCH]
    lag = ((place + HALF) % PATCH) - HALF
    full = (basis * lag) @ basis.T
    form = np.zeros((HALF, PATCH))
    form[1:] = 2 * full[HALF + 1 :]
    form[1:, HALF + 1 :] = 0
    form[0, :HALF] = basis[:HALF, HALF]
    basis_high, basis_low = split_table(basis)
    form_high, form_low = split_table(form)

    def side_by_side(part):
        out = np.zeros((2 * PATCH, 2 * PATCH), ml_dtypes.bfloat16)
        for t in range(2):
            for s in range(2):
                out[t * PATCH : (t + 1) * PATCH, s * PATCH + t * HALF : s * PATCH + (t + 1) * HALF] = (
                    part[s * HALF : (s + 1) * HALF].T
                )
        return out

    def columns(part):
        out = np.zeros((2 * PATCH, PATCH), ml_dtypes.bfloat16)
        for t in range(2):
            for s in range(2):
                out[s * PATCH + t * HALF : s * PATCH + (t + 1) * HALF, t * HALF : (t + 1) * HALF] = (
                    part[:, s * HALF : (s + 1) * HALF].T
                )
        return out

    along = np.stack([side_by_side(basis_high), side_by_side(basis_low)])
    down = np.concatenate(
        [np.concatenate([basis_high, basis_high], 1), np.concatenate([basis_low, basis_low * 0], 1)], 0
    )
    form_rows = np.concatenate(
        [np.concatenate([form_high, form_high], 1), np.concatenate([form_low, form_low * 0], 1)], 0
    )
    form_cols = np.concatenate([columns(form_high), columns(form_low)], 1)
    return along, down, form_rows, form_cols


def dot(a, b):
    return jnp.dot(a, b, preferred_element_type=F32)


def split(x):
    high = x.astype(BF)
    return high, (x - high.astype(F32)).astype(BF)


def fill_padded(padded, image_ref, low_ref, high_ref):
    rows, cols = image_ref.shape
    padded[:, 0:LANES] = jnp.zeros((padded.shape[0], LANES), F32)
    padded[:, LANES + cols :] = jnp.zeros((padded.shape[0], LANES), F32)
    padded[2 * OFFMAX + rows :, :] = jnp.zeros((8, padded.shape[1]), F32)
    padded[0:OFFMAX, LANES : LANES + cols] = low_ref[...].astype(F32)
    padded[OFFMAX + rows : 2 * OFFMAX + rows, LANES : LANES + cols] = high_ref[...].astype(F32)

    def step(i, carry):
        r = pl.multiple_of(i * 64, 64)
        padded[pl.ds(r + OFFMAX, 64), LANES : LANES + cols] = image_ref[pl.ds(r, 64), :].astype(F32)
        return carry

    lax.fori_loop(0, rows // 64, step, 0)


def fill_windows(window, padded, off_ref, s, c, rows):
    lane = lax.broadcasted_iota(jnp.int32, (PATCH + 8, LANES), 1)

    def step(i, carry):
        for t in range(2):
            j = 2 * c + t
            oy = off_ref[s, 0, i, j]
            ox = off_ref[s, 1, i, j]
            left = (ox < 0).astype(jnp.int32)
            base = pl.multiple_of((j + 1 - left) * LANES, LANES)
            shift = ox + LANES * left
            top = OFFMAX + oy
            aligned = pl.multiple_of(i * PATCH + (top // 8) * 8, 8)
            block = padded[pl.ds(aligned, PATCH + 8), pl.ds(base, 2 * LANES)]
            turn = jnp.bitwise_and(LANES - shift, LANES - 1)
            first = pltpu.roll(block[:, :LANES], turn, 1)
            second = pltpu.roll(block[:, LANES:], turn, 1)
            cut = jnp.where(lane < LANES - shift, first, second)
            cut = pltpu.roll(cut, PATCH + 8 - top % 8, 0)[:PATCH]
            window[pl.ds(pl.multiple_of(i * PATCH, PATCH), PATCH), t * LANES : (t + 1) * LANES] = cut.astype(BF)
        return carry

    lax.fori_loop(0, rows, step, 0)


def transform(block, along_ref, down_ref):
    part = dot(block, along_ref[0]) + dot(block, along_ref[1])
    high, low = split(part)
    both = dot(down_ref[...], jnp.concatenate([high, low], 0))
    return both[:PATCH] + both[PATCH:]


def store_coefficients(out_ref, coef):
    row = lax.broadcasted_iota(jnp.int32, (8, LANES), 0)
    lane = lax.broadcasted_iota(jnp.int32, (8, LANES), 1)
    corner = jnp.logical_and(row == 0, lane % HALF == 0)
    out_ref[...] = coef
    mean = 0.25 * (
        coef[0:8, :LANES] + coef[0:8, LANES:] + coef[HALF : HALF + 8, :LANES] + coef[HALF : HALF + 8, LANES:]
    )
    mean = jnp.where(corner, mean, 0.0)
    for r in (0, HALF):
        for q in (0, LANES):
            out_ref[r : r + 8, q : q + LANES] = coef[r : r + 8, q : q + LANES] - mean


def own_kernel(off_ref, image_ref, low_ref, high_ref, along_ref, down_ref, patch_out, window_out, padded, window):
    s, c = pl.program_id(0), pl.program_id(1)
    rows = image_ref.shape[0] // PATCH

    @pl.when(c == 0)
    def _():
        fill_padded(padded, image_ref, low_ref, high_ref)

    fill_windows(window, padded, off_ref, s, c, rows)
    lanes = pl.ds(pl.multiple_of(c * 2 * LANES, 2 * LANES), 2 * LANES)

    def step(i, carry):
        down = pl.ds(pl.multiple_of(i * PATCH, PATCH), PATCH)
        store_coefficients(patch_out.at[i], transform(image_ref[down, lanes], along_ref, down_ref))
        store_coefficients(window_out.at[i], transform(window[down, :], along_ref, down_ref))
        return carry

    lax.fori_loop(0, rows, step, 0, unroll=2)


def correlate(a_ref, b_ref, coef, pieces, rows_ref, cols_ref):
    lane = lax.broadcasted_iota(jnp.int32, (16, LANES), 1)
    row = lax.broadcasted_iota(jnp.int32, (16, LANES), 0)
    sign_j = jnp.where(lane % HALF == 0, -1.0, 1.0).astype(F32)
    first_row = jnp.where(row == 0, -1.0, 1.0).astype(F32)
    total = jnp.zeros((16, LANES), F32)
    for g in range(HALF // 16):
        top, bottom = slice(16 * g, 16 * g + 16), slice(HALF + 16 * g, HALF + 16 * g + 16)
        acc, acs, asc, ass = a_ref[top, :LANES], a_ref[top, LANES:], a_ref[bottom, :LANES], a_ref[bottom, LANES:]
        bcc, bcs, bsc, bss = b_ref[top, :LANES], b_ref[top, LANES:], b_ref[bottom, :LANES], b_ref[bottom, LANES:]
        acs_j, ass_j = acs * sign_j, ass * sign_j
        cc = acc * bcc + acs * bcs + asc * bsc + ass * bss
        cs = acc * bcs + asc * bss - (acs_j * bcc + ass_j * bsc)
        turned_sc = asc * bcc + ass * bcs
        turned_ss = asc * bcs - ass_j * bcc
        if g == 0:
            turned_sc, turned_ss = turned_sc * first_row, turned_ss * first_row
        sc = acc * bsc + acs * bss - turned_sc
        ss = acc * bss - acs_j * bsc - turned_ss
        total = total + (cc * cc + cs * cs + sc * sc + ss * ss)
        for where, lanes, value in (
            (top, slice(0, LANES), cc),
            (top, slice(LANES, 2 * LANES), cs),
            (bottom, slice(0, LANES), sc),
            (bottom, slice(LANES, 2 * LANES), ss),
        ):
            high, low = split(value)
            coef[where, lanes] = value
            pieces[where, lanes] = high
            pieces[slice(PATCH + where.start, PATCH + where.stop), lanes] = low
    down = dot(rows_ref[...], pieces[...])
    down = down[:HALF] + down[HALF:]
    across = dot(pieces[...], cols_ref[...])
    across = across[:PATCH, :LANES] + across[:PATCH, LANES:] + across[PATCH:, :LANES]
    row8 = lax.broadcasted_iota(jnp.int32, (8, 2 * LANES), 0)
    head = down[0:8]
    moment_r = jnp.where(row8 == 0, -float(HALF) * head, coef[HALF : HALF + 8, :]) * head
    for g in range(1, HALF // 8):
        moment_r = moment_r + down[8 * g : 8 * g + 8] * coef[HALF + 8 * g : HALF + 8 * g + 8, :]
    moment_r = moment_r[:, :LANES] + moment_r[:, LANES:]
    lane8 = lax.broadcasted_iota(jnp.int32, (8, LANES), 1) % HALF == 0
    moment_c = jnp.zeros((8, LANES), F32)
    for g in range(PATCH // 8):
        piece = across[8 * g : 8 * g + 8]
        other = jnp.where(lane8, -float(HALF) * piece, coef[8 * g : 8 * g + 8, LANES:])
        moment_c = moment_c + other * piece
    add = lambda x: jnp.sum(x, axis=0, keepdims=True)
    return add(total), add(moment_r), add(moment_c)


def pair_kernel(
    place_ref, off_ref, image_ref, low_ref, high_ref, along_ref, down_ref, rows_ref, cols_ref,
    own_patch, own_window, fwd_ref, bwd_ref, valid_ref, flow_out, tile_out,
    padded, window, left, right, coef, pieces, sums,
):
    s, c = pl.program_id(0), pl.program_id(1)
    rows = image_ref.shape[0] // PATCH
    pairs = pl.num_programs(1)

    @pl.when(c == 0)
    def _():
        fill_padded(padded, image_ref, low_ref, high_ref)

    fill_windows(window, padded, off_ref, s, c, rows)
    lanes = pl.ds(pl.multiple_of(c * 2 * LANES, 2 * LANES), 2 * LANES)

    def step(i, carry):
        down = pl.ds(pl.multiple_of(i * PATCH, PATCH), PATCH)
        store_coefficients(left, transform(image_ref[down, lanes], along_ref, down_ref))
        store_coefficients(right, transform(window[down, :], along_ref, down_ref))
        forward = correlate(own_patch.at[i], right, coef.at[0], pieces.at[0], rows_ref, cols_ref)
        backward = correlate(left, own_window.at[i], coef.at[1], pieces.at[1], rows_ref, cols_ref)
        for k, value in enumerate(forward + backward):
            sums[k, c, pl.ds(i, 1), :] = value
        return carry

    lax.fori_loop(0, rows, step, 0)

    @pl.when(c == pairs - 1)
    def _():
        count = 2 * sums.shape[1]
        lane = lax.broadcasted_iota(jnp.int32, (rows, LANES), 1)
        gathered = []
        for k in range(6):
            value = jnp.zeros((rows, LANES), F32)
            for p in range(sums.shape[1]):
                held = sums[k, p]
                for t in range(2):
                    mine = (lane >= HALF) if t else (lane < HALF)
                    value = jnp.where(
                        lane == 2 * p + t, jnp.sum(jnp.where(mine, held, 0.0), axis=1, keepdims=True), value
                    )
            gathered.append(value[:, :count])
        scale = (2.0 / PATCH) ** 4 * HALF * HALF
        lag_scale = scale / HALF
        eps = PATCH * PATCH * 1e-6
        notlast = place_ref[s].astype(F32)
        weight = valid_ref[...].astype(F32) * notlast
        flows = []
        for comp in range(2):
            fwd = gathered[1 + comp] * lag_scale / (gathered[0] * scale + eps) + fwd_ref[comp].astype(F32)
            bwd = gathered[4 + comp] * lag_scale / (gathered[3] * scale + eps) + bwd_ref[comp].astype(F32)
            flow = 0.5 * (fwd - bwd) * notlast
            flow_out[comp] = flow
            flows.append(flow)
        fill = jnp.zeros((rows, LANES - 4 * count), F32)
        tile_out[...] = jnp.concatenate(flows + [weight, weight, fill], axis=1)


def mesh_kernel(place_ref, all_ref, shift_out, held):
    sections, height, _ = all_ref.shape
    sec_dev, _, rows, count = shift_out.shape
    lane = lax.broadcasted_iota(jnp.int32, (1, height, LANES), 2)
    down = lax.broadcasted_iota(jnp.int32, (1, height, LANES), 1)
    used = lane < 2 * count
    first = lane < count
    everything = all_ref[...]
    flow = jnp.where(used, everything, 0.0)
    weight = jnp.where(used, pltpu.roll(everything, LANES - 2 * count, 2), 0.0)
    pulled = weight * flow
    counts = jnp.sum(jnp.sum(jnp.where(first, weight, 0.0), axis=1, keepdims=True), axis=2, keepdims=True)
    weighted = jnp.sum(pulled, axis=1, keepdims=True)
    lane1 = lax.broadcasted_iota(jnp.int32, (1, 1, LANES), 2)
    sum_y = jnp.sum(jnp.where(lane1 < count, weighted, 0.0), axis=2, keepdims=True)
    sum_x = jnp.sum(jnp.where(lane1 >= count, weighted, 0.0), axis=2, keepdims=True)
    many = jnp.maximum(counts, 1.0)
    mean = jnp.where(first, sum_y / many, sum_x / many)
    starts = []
    start = jnp.zeros((1, height, LANES), F32)
    for k in range(sections):
        starts.append(start)
        start = start + mean[k : k + 1]
    shift = jnp.concatenate(starts, 0)
    zero = jnp.zeros((1, height, LANES), F32)
    col = lane % count
    has_left, has_right = (col > 0).astype(F32), (col < count - 1).astype(F32)
    has_up, has_down = (down > 0).astype(F32), (down < height - 1).astype(F32)
    degree = has_left + has_right + has_up + has_down
    for _ in range(ITERS):
        plane = (
            has_up * pltpu.roll(shift, 1, 1)
            + has_down * pltpu.roll(shift, height - 1, 1)
            + has_left * pltpu.roll(shift, 1, 2)
            + has_right * pltpu.roll(shift, LANES - 1, 2)
            - degree * shift
        )
        after = jnp.concatenate([shift[1:], zero], 0)
        spring = weight * (after - shift) - pulled
        between = spring - jnp.concatenate([zero, spring[:-1]], 0)
        shift = shift + 0.25 * (plane + between)
    held[...] = shift
    for k in range(sec_dev):
        mine = held[place_ref[0] + k, pl.ds(pl.multiple_of(place_ref[1], 8), rows), :]
        shift_out[k, 0] = mine[:, :count]
        shift_out[k, 1] = mine[:, count : 2 * count]


def section_spec(shape):
    return pl.BlockSpec((None,) + shape[1:], lambda s, c: (s,) + (0,) * (len(shape) - 1))


def whole_spec(shape):
    return pl.BlockSpec(shape, lambda s, c: (0,) * len(shape))


SCALARS = pl.BlockSpec(memory_space=pltpu.SMEM)


def body(image, fwd_offset, bwd_offset, valid):
    sec_dev, height, width = image.shape
    rows, count = valid.shape[1:]
    pairs = count // 2
    sec_size, tile_size = lax.axis_size("sec"), lax.axis_size("tile")
    sections = sec_dev * sec_size
    along, down, form_rows, form_cols = (jnp.asarray(t) for t in tables())

    earlier = [(i, i - 1) for i in range(1, sec_size)]
    arriving = lax.ppermute(image[:1], "sec", earlier)
    up = [(i, i + 1) for i in range(tile_size - 1)]
    back = [(i + 1, i) for i in range(tile_size - 1)]
    low = lax.ppermute(image[:, -OFFMAX:], "tile", up)
    high = lax.ppermute(image[:, :OFFMAX], "tile", back)
    edges = lax.ppermute(jnp.concatenate([low[:1], high[:1]], 1), "sec", earlier)
    after = jnp.concatenate([image[1:], arriving], 0)
    after_low = jnp.concatenate([low[1:], edges[:, :OFFMAX]], 0)
    after_high = jnp.concatenate([high[1:], edges[:, OFFMAX:]], 0)

    coef_shape = jax.ShapeDtypeStruct((sec_dev, pairs, rows, PATCH, 2 * PATCH), F32)
    coef_spec = pl.BlockSpec((None, None, rows, PATCH, 2 * PATCH), lambda s, c: (s, c, 0, 0, 0))
    padded = pltpu.VMEM((height + 2 * OFFMAX + 8, width + 2 * LANES), F32)
    window = pltpu.VMEM((height, 2 * LANES), BF)
    own_patch, own_window = pl.pallas_call(
        own_kernel,
        grid=(sec_dev, pairs),
        out_shape=(coef_shape, coef_shape),
        in_specs=[
            SCALARS,
            section_spec(image.shape),
            section_spec(low.shape),
            section_spec(high.shape),
            whole_spec(along.shape),
            whole_spec(down.shape),
        ],
        out_specs=(coef_spec, coef_spec),
        scratch_shapes=[padded, window],
        compiler_params=pltpu.CompilerParams(vmem_limit_bytes=48 * 1024 * 1024),
        cost_estimate=pl.CostEstimate(flops=10**10, bytes_accessed=10**7, transcendentals=0),
        name="own_spectra",
    )(bwd_offset, image, low, high, along, down)

    place = lax.axis_index("sec") * sec_dev
    notlast = (place + jnp.arange(sec_dev, dtype=jnp.int32) < sections - 1).astype(jnp.int32)
    flow_shape = jax.ShapeDtypeStruct((sec_dev, 2, rows, count), F32)
    pair_flow, tile = pl.pallas_call(
        pair_kernel,
        grid=(sec_dev, pairs),
        out_shape=(flow_shape, jax.ShapeDtypeStruct((sec_dev, rows, LANES), F32)),
        in_specs=[
            SCALARS,
            SCALARS,
            section_spec(after.shape),
            section_spec(after_low.shape),
            section_spec(after_high.shape),
            whole_spec(along.shape),
            whole_spec(down.shape),
            whole_spec(form_rows.shape),
            whole_spec(form_cols.shape),
            coef_spec,
            coef_spec,
            section_spec(fwd_offset.shape),
            section_spec(bwd_offset.shape),
            section_spec(valid.shape),
        ],
        out_specs=(section_spec(flow_shape.shape), section_spec((sec_dev, rows, LANES))),
        scratch_shapes=[
            padded,
            window,
            pltpu.VMEM((PATCH, 2 * PATCH), F32),
            pltpu.VMEM((PATCH, 2 * PATCH), F32),
            pltpu.VMEM((2, PATCH, 2 * PATCH), F32),
            pltpu.VMEM((2, 2 * PATCH, 2 * PATCH), BF),
            pltpu.VMEM((6, pairs, rows, LANES), F32),
        ],
        compiler_params=pltpu.CompilerParams(vmem_limit_bytes=48 * 1024 * 1024),
        cost_estimate=pl.CostEstimate(flops=10**10, bytes_accessed=10**7, transcendentals=0),
        name="pair_flows",
    )(notlast, fwd_offset, after, after_low, after_high, along, down, form_rows, form_cols,
      own_patch, own_window, fwd_offset, bwd_offset, valid)

    devices = sec_size * tile_size
    everywhere = lax.all_to_all(jnp.broadcast_to(tile[None], (devices,) + tile.shape), ("sec", "tile"), 0, 0)
    everywhere = (
        everywhere.reshape(sec_size, tile_size, sec_dev, rows, LANES)
        .transpose(0, 2, 1, 3, 4)
        .reshape(sections, tile_size * rows, LANES)
    )
    where = jnp.stack([place, lax.axis_index("tile") * rows]).astype(jnp.int32)
    mesh_shift = pl.pallas_call(
        mesh_kernel,
        out_shape=flow_shape,
        in_specs=[SCALARS, pl.BlockSpec(memory_space=pltpu.VMEM)],
        out_specs=pl.BlockSpec(memory_space=pltpu.VMEM),
        scratch_shapes=[pltpu.VMEM((sections, tile_size * rows, LANES), F32)],
        name="relax",
    )(where, everywhere)
    return pair_flow, mesh_shift


def solution(mesh):
    return jax.shard_map(
        body,
        mesh=mesh,
        in_specs=(
            P("sec", "tile", None),
            P("sec", None, "tile", None),
            P("sec", None, "tile", None),
            P("sec", "tile", None),
        ),
        out_specs=(P("sec", None, "tile", None), P("sec", None, "tile", None)),
        check_vma=False,
    )
```

time: 428 us -> 88 us (0.21); the launches traced: 420 us -> 87.6 us
  matrix products: 283 us -> 0 us
  Pallas kernels: 0 us -> 52.6 us
  local copies, waits for them, and re-layouts: 42.2 us -> 6.29 us
  starting transfers between devices: 38.9 us -> 14.8 us
  blocking collectives: 23.3 us -> 0 us
  other arithmetic: 20 us -> 0.59 us
    dot_general x38 -> x0, matrix products: 283 us -> none  [the longest x4 34.5 us: spectrum(): jnp.einsum('nuk,kv->nuv', left_cosine, cosine_table, precision=highest_peak)]
    pallas_call x0 -> x3, Pallas kernels: none -> 52.6 us  [the longest x1 33.3 us: body(): pl.pallas_call(pair_kernel, grid=(sec_dev, pairs), out_shape=(flow_shape,...]
    slice x18 -> x2, local copies, waits for them, and re-layouts: 36.8 us -> 0.79 us  [the longest x1 0.78 us: body(): low = lax.ppermute(image[:, -OFFMAX:], 'tile', up)]
    ppermute x15 -> x4, starting transfers between devices: 38.9 us -> 8.78 us  [the longest x1 4.92 us: body(): low = lax.ppermute(image[:, -OFFMAX:], 'tile', up)]
    concatenate x10 -> x1, other arithmetic: 14.1 us -> 0.01 us  [body(): jnp.concatenate([low[:1], high[:1]], 1)]
    psum x1 -> x0, blocking collectives: 13.7 us -> none  [body(): lax.psum((jnp.sum(weight[:, None] * pair_flow, axis=(2, 3)), jnp.sum(weig...]
    all_gather x1 -> x0, blocking collectives: 9.69 us -> none  [entering(): everything = lax.all_gather(array, axis)]
    all_to_all x0 -> x1, waiting for transfers between devices: none -> 7.81 us  [body(): lax.all_to_all(jnp.broadcast_to(tile[None], (devices,) + tile.shape), ('s...]
  transfers between devices with their start and end apart: 15 -> 5, of which waited for: 6 -> 3; matrix products, arithmetic and copies ran while one was open for 17% -> 2% of each run, Pallas kernels for 0% -> 20%
where the time goes in v1:
time: 88 us; the launch traced here: 87.6 us
  Pallas kernels  52.6 us (60%)
  starting transfers between devices  14.8 us (17%)
  waiting for transfers between devices  12.5 us (14%)
  local copies, waits for them, and re-layouts  6.29 us (7%)
    pallas_call x1, Pallas kernels, body(): pl.pallas_call(pair_kernel, grid=(sec_dev, pairs), out_shape=(flow_shape,...  33.3 us
    pallas_call x1, Pallas kernels, body(): pl.pallas_call(own_kernel, grid=(sec_dev, pairs), out_shape=(coef_shape,...  17.2 us
    all_to_all x1, waiting for transfers between devices, body(): lax.all_to_all(jnp.broadcast_to(tile[None], (devices,) + tile.shape), ('s...  7.81 us
    all_to_all x1, starting transfers between devices, body(): lax.all_to_all(jnp.broadcast_to(tile[None], (devices,) + tile.shape), ('s...  6 us
    ppermute x1, starting transfers between devices, body(): low = lax.ppermute(image[:, -OFFMAX:], 'tile', up)  4.92 us
    unnamed x18, local copies, waits for them, and re-layouts  4.82 us
    ppermute x1, waiting for transfers between devices, body(): high = lax.ppermute(image[:, :OFFMAX], 'tile', back)  4.43 us
    pallas_call x1, Pallas kernels, body(): pl.pallas_call(mesh_kernel, out_shape=flow_shape, in_specs=[SCALARS, pl.B...  2.05 us
  transfers between devices with their start and end apart: 5, of which 3 were waited for; matrix products, arithmetic and copies ran while one was open for 2% of the time, Pallas kernels for 20%

profile of v1, /device:TPU:0, one launch (start us, length us, event | category | flops | bytes accessed | tf_op | source)
XLA Modules:
  0.0 87.6 jit_solution(12550611156800683592)
XLA Ops:
  0.6 1.3 %collective-permute-start = (bf16[1,1024,1024]{2,1,0:T(8,128)(2,1)}, bf16[1,1024,1024]{2,1,0:T(8,128)(2,1)S(1)}, u32[]{:S(2)}, u32[]{:S(2)}) collective-permute-start(bf16[1,1024,1024]{2,1,0:T(8,128)(2,1)} %image_ref.1), channel_id=1, source_target_pairs={{4,0},{8,4},{12,8},{16,12},{20,16},{24,20},{28,24},{5,1},{9,5},{13... | collective-permute-start | bytes 6291464 | tf_op jit(solution)/shard_map/ppermute | solution.py:345
  1.9 0.8 fusion
  2.7 4.9 %collective-permute-start.1 = (bf16[1,16,1024]{2,1,0:T(8,128)(2,1)S(1)}, bf16[1,16,1024]{2,1,0:T(8,128)(2,1)S(1)}, u32[]{:S(2)}, u32[]{:S(2)}) collective-permute-start(bf16[1,16,1024]{2,1,0:T(8,128)(2,1)S(1)} %get-tuple-element.10), channel_id=1, source_target_pairs={{0,1},{1,2},{2,3},{4,5},{5,6},{6,7},{8,9},{9,10},{10,11},{12,13},{... | collective-permute-start | bytes 98312 | tf_op jit(solution)/shard_map/ppermute | solution.py:348
  7.6 1.3 %collective-permute-start.2 = (bf16[1,16,1024]{2,1,0:T(8,128)(2,1)S(1)}, bf16[1,16,1024]{2,1,0:T(8,128)(2,1)S(1)}, u32[]{:S(2)}, u32[]{:S(2)}) collective-permute-start(bf16[1,16,1024]{2,1,0:T(8,128)(2,1)S(1)} %get-tuple-element.11), channel_id=1, source_target_pairs={{1,0},{2,1},{3,2},{5,4},{6,5},{7,6},{9,8},{10,9},{11,10},{13,12},{... | collective-permute-start | bytes 98312 | tf_op jit(solution)/shard_map/ppermute | solution.py:349
  8.9 0.3 collective-permute-done.1.low_ref
  9.2 4.4 %collective-permute-done.2.high_ref = bf16[1,16,1024]{2,1,0:T(8,128)(2,1)S(1)} collective-permute-done((bf16[1,16,1024]{2,1,0:T(8,128)(2,1)S(1)}, bf16[1,16,1024]{2,1,0:T(8,128)(2,1)S(1)}, u32[]{:S(2)}, u32[]{:S(2)}) %collective-permute-start.2) | collective-permute-done | bytes 32800 | tf_op jit(solution)/shard_map/ppermute | solution.py:349
  13.7 1.3 %collective-permute-start.3 = (bf16[1,32,1024]{2,1,0:T(8,128)(2,1)S(1)}, bf16[1,32,1024]{2,1,0:T(8,128)(2,1)S(1)}, u32[]{:S(2)}, u32[]{:S(2)}) collective-permute-start(bf16[1,32,1024]{2,1,0:T(8,128)(2,1)S(1)} %pad_maximum_fusion), channel_id=1, source_target_pairs={{4,0},{8,4},{12,8},{16,12},{20,16},{24,20},{28,24},{5,1},{9,5},{13... | collective-permute-start | bytes 196616 | tf_op jit(solution)/shard_map/ppermute | solution.py:350
  15.0 0.0 copy-start
  15.0 1.6 %copy-done = bf16[1,1024,1024]{2,1,0:T(8,128)(2,1)S(1)} copy-done((bf16[1,1024,1024]{2,1,0:T(8,128)(2,1)S(1)}, bf16[1,1024,1024]{2,1,0:T(8,128)(2,1)}, u32[]{:S(2)}) %copy-start) | copy-done | bytes 2097176
  16.6 0.0 copy-start.2
  16.6 0.7 copy-done.2
  17.3 0.0 copy-start.4
  17.3 0.9 %copy-done.4 = bf16[2,256,256]{2,1,0:T(8,128)(2,1)S(1)} copy-done((bf16[2,256,256]{2,1,0:T(8,128)(2,1)S(1)}, bf16[2,256,256]{2,1,0:T(8,128)(2,1)}, u32[]{:S(2)}) %copy-start.4) | copy-done | bytes 262168
  18.2 0.0 copy-start.5
  18.2 0.9 %copy-done.5 = bf16[256,256]{1,0:T(8,128)(2,1)S(1)} copy-done((bf16[256,256]{1,0:T(8,128)(2,1)S(1)}, bf16[256,256]{1,0:T(8,128)(2,1)}, u32[]{:S(2)}) %copy-start.5) | copy-done | bytes 131096
  19.1 0.0 copy-start.1
  19.1 0.0 copy-start.3
  19.1 0.0 copy-start.6
  19.1 17.2 %own_spectra.1 = (f32[1,4,8,128,256]{4,3,2,1,0:T(8,128)}, f32[1,4,8,128,256]{4,3,2,1,0:T(8,128)}) custom-call(s32[1,2,8,8]{3,2,1,0:T(8,128)S(1)} %copy-done.2, bf16[1,1024,1024]{2,1,0:T(8,128)(2,1)S(1)} %copy-done, bf16[1,16,1024]{2,1,0:T(8,128)(2,1)S(1)} %collective-permute-done.1.low_ref, bf16[1,16,1024]{2,1,0:T(8,128)(2,1)S(1)} %collective-permute-done.2.high_ref, ...), custom_call_target="tpu_custom_call" | custom-call | flops 10000000000 | bytes 10000000 | tf_op jit(solution)/shard_map/own_spectra/pallas_call | solution.py:359
  36.4 0.0 collective-permute-done.3
  36.4 0.0 collective-permute-done.image_ref
  36.4 0.0 copy-done.1
  36.4 0.0 copy-done.3
  36.4 0.0 copy-done.6
  36.4 0.0 copy-done.7
  36.4 33.3 %pair_flows.1 = (f32[1,2,8,8]{3,2,1,0:T(8,128)}, f32[1,8,128]{2,1,0:T(8,128)S(1)}) custom-call(s32[1]{0:T(128)S(6)} %convert_element_type.3.place_ref, s32[1,2,8,8]{3,2,1,0:T(8,128)S(1)} %copy-done.1, bf16[1,1024,1024]{2,1,0:T(8,128)(2,1)S(1)} %collective-permute-done.image_ref, bf16[1,16,1024]{2,1,0:T(8,128)(2,1)S(1)} %get-tuple-element.13.low_ref, ...), custom_call_target="tpu_custom_call" | custom-call | flops 10000000000 | bytes 10000000 | tf_op jit(solution)/shard_map/pair_flows/pallas_call | solution.py:381
  69.8 0.7 broadcast_in_dim.9
  70.4 6.0 %all-to-all-start = ((f32[32,1,8,128]{3,2,1,0:T(8,128)}), f32[32,1,8,128]{3,2,1,0:T(8,128)S(1)}, u32[]{:S(2)}, u32[]{:S(2)}) async-start(f32[32,1,8,128]{3,2,1,0:T(8,128)} %broadcast_in_dim.9), calls=%async_computation | async-start | bytes 262144 | tf_op jit(solution)/shard_map/all_to_all | solution.py:418
  76.5 0.6 pad_add_fusion.place_ref
  77.0 7.8 %all-to-all-done = f32[32,1,8,128]{3,2,1,0:T(8,128)S(1)} async-done(((f32[32,1,8,128]{3,2,1,0:T(8,128)}), f32[32,1,8,128]{3,2,1,0:T(8,128)S(1)}, u32[]{:S(2)}, u32[]{:S(2)}) %all-to-all-start) | async-done | bytes 131104 | tf_op jit(solution)/shard_map/all_to_all | solution.py:418
  84.9 0.7 copy-done.8
  85.5 2.0 %relax.1 = f32[1,2,8,8]{3,2,1,0:T(8,128)} custom-call(s32[2]{0:T(128)} %pad_add_fusion.place_ref, f32[8,32,128]{2,1,0:T(8,128)} %bitcast.5), custom_call_target="tpu_custom_call" | custom-call | tf_op jit(solution)/shard_map/relax/pallas_call | solution.py:425
  (4 shorter events, 0.0 us)
Async XLA Ops:
  0.6 35.7 %collective-permute-start = (bf16[1,1024,1024]{2,1,0:T(8,128)(2,1)}, bf16[1,1024,1024]{2,1,0:T(8,128)(2,1)S(1)}, u32[]{:S(2)}, u32[]{:S(2)}) collective-permute-start(bf16[1,1024,1024]{2,1,0:T(8,128)(2,1)} %image_ref.1), channel_id=1, source_target_pairs={{4,0},{8,4},{12,8},{16,12},{20,16},{24,20},{28,24},{5,1},{9,5},{13... | collective-permute-start | bytes 6291464 | tf_op jit(solution)/shard_map/ppermute | solution.py:345
  2.7 6.5 %collective-permute-start.1 = (bf16[1,16,1024]{2,1,0:T(8,128)(2,1)S(1)}, bf16[1,16,1024]{2,1,0:T(8,128)(2,1)S(1)}, u32[]{:S(2)}, u32[]{:S(2)}) collective-permute-start(bf16[1,16,1024]{2,1,0:T(8,128)(2,1)S(1)} %get-tuple-element.10), channel_id=1, source_target_pairs={{0,1},{1,2},{2,3},{4,5},{5,6},{6,7},{8,9},{9,10},{10,11},{12,13},{... | collective-permute-start | bytes 98312 | tf_op jit(solution)/shard_map/ppermute | solution.py:348
  7.6 6.0 %collective-permute-start.2 = (bf16[1,16,1024]{2,1,0:T(8,128)(2,1)S(1)}, bf16[1,16,1024]{2,1,0:T(8,128)(2,1)S(1)}, u32[]{:S(2)}, u32[]{:S(2)}) collective-permute-start(bf16[1,16,1024]{2,1,0:T(8,128)(2,1)S(1)} %get-tuple-element.11), channel_id=1, source_target_pairs={{1,0},{2,1},{3,2},{5,4},{6,5},{7,6},{9,8},{10,9},{11,10},{13,12},{... | collective-permute-start | bytes 98312 | tf_op jit(solution)/shard_map/ppermute | solution.py:349
  13.7 22.7 %collective-permute-start.3 = (bf16[1,32,1024]{2,1,0:T(8,128)(2,1)S(1)}, bf16[1,32,1024]{2,1,0:T(8,128)(2,1)S(1)}, u32[]{:S(2)}, u32[]{:S(2)}) collective-permute-start(bf16[1,32,1024]{2,1,0:T(8,128)(2,1)S(1)} %pad_maximum_fusion), channel_id=1, source_target_pairs={{4,0},{8,4},{12,8},{16,12},{20,16},{24,20},{28,24},{5,1},{9,5},{13... | collective-permute-start | bytes 196616 | tf_op jit(solution)/shard_map/ppermute | solution.py:350
  15.0 1.6 %copy-start = (bf16[1,1024,1024]{2,1,0:T(8,128)(2,1)S(1)}, bf16[1,1024,1024]{2,1,0:T(8,128)(2,1)}, u32[]{:S(2)}) copy-start(bf16[1,1024,1024]{2,1,0:T(8,128)(2,1)} %image_ref.1) | copy-start | bytes 6291460
  16.6 0.7 copy-start.2
  17.3 0.9 %copy-start.4 = (bf16[2,256,256]{2,1,0:T(8,128)(2,1)S(1)}, bf16[2,256,256]{2,1,0:T(8,128)(2,1)}, u32[]{:S(2)}) copy-start(bf16[2,256,256]{2,1,0:T(8,128)(2,1)} %constant.21.clone.along_ref) | copy-start | bytes 786436
  18.2 0.9 %copy-start.5 = (bf16[256,256]{1,0:T(8,128)(2,1)S(1)}, bf16[256,256]{1,0:T(8,128)(2,1)}, u32[]{:S(2)}) copy-start(bf16[256,256]{1,0:T(8,128)(2,1)} %constant.22.clone.down_ref) | copy-start | bytes 393220
  19.1 17.3 %copy-start.1 = (s32[1,2,8,8]{3,2,1,0:T(8,128)S(1)}, s32[1,2,8,8]{3,2,1,0:T(8,128)}, u32[]{:S(2)}) copy-start(s32[1,2,8,8]{3,2,1,0:T(8,128)} %fwd_ref.1) | copy-start | bytes 1540
  19.1 17.3 %copy-start.3 = (s32[1,8,8]{2,1,0:T(8,128)S(1)}, s32[1,8,8]{2,1,0:T(8,128)}, u32[]{:S(2)}) copy-start(s32[1,8,8]{2,1,0:T(8,128)} %valid_ref.1) | copy-start | bytes 772
  19.1 17.3 %copy-start.6 = (bf16[256,256]{1,0:T(8,128)(2,1)S(1)}, bf16[256,256]{1,0:T(8,128)(2,1)}, u32[]{:S(2)}) copy-start(bf16[256,256]{1,0:T(8,128)(2,1)} %constant.24.clone.cols_ref) | copy-start | bytes 393220
  19.1 17.3 %copy-start.7 = (bf16[128,256]{1,0:T(8,128)(2,1)S(1)}, bf16[128,256]{1,0:T(8,128)(2,1)}, u32[]{:S(2)}) copy-start(bf16[128,256]{1,0:T(8,128)(2,1)} %constant.23.clone.rows_ref) | copy-start | bytes 196612
  70.4 14.4 %all-to-all-start = ((f32[32,1,8,128]{3,2,1,0:T(8,128)}), f32[32,1,8,128]{3,2,1,0:T(8,128)S(1)}, u32[]{:S(2)}, u32[]{:S(2)}) async-start(f32[32,1,8,128]{3,2,1,0:T(8,128)} %broadcast_in_dim.9), calls=%async_computation | async-start | bytes 262144 | tf_op jit(solution)/shard_map/all_to_all | solution.py:418
  84.9 0.7 copy-start.8

commit v2 on v1

--- a/solution.py
+++ b/solution.py
@@ -63,7 +63,7 @@
                 )
         return out
 
-    along = np.stack([side_by_side(basis_high), side_by_side(basis_low)])
+    along = np.concatenate([side_by_side(basis_high), side_by_side(basis_low)], 0)
     down = np.concatenate(
         [np.concatenate([basis_high, basis_high], 1), np.concatenate([basis_low, basis_low * 0], 1)], 0
     )
@@ -99,35 +99,37 @@
     lax.fori_loop(0, rows // 64, step, 0)
 
 
-def fill_windows(window, padded, off_ref, s, c, rows):
+def fill_window_row(window, padded, off_ref, s, c, i):
     lane = lax.broadcasted_iota(jnp.int32, (PATCH + 8, LANES), 1)
-
-    def step(i, carry):
-        for t in range(2):
-            j = 2 * c + t
-            oy = off_ref[s, 0, i, j]
-            ox = off_ref[s, 1, i, j]
-            left = (ox < 0).astype(jnp.int32)
-            base = pl.multiple_of((j + 1 - left) * LANES, LANES)
-            shift = ox + LANES * left
-            top = OFFMAX + oy
-            aligned = pl.multiple_of(i * PATCH + (top // 8) * 8, 8)
-            block = padded[pl.ds(aligned, PATCH + 8), pl.ds(base, 2 * LANES)]
-            turn = jnp.bitwise_and(LANES - shift, LANES - 1)
-            first = pltpu.roll(block[:, :LANES], turn, 1)
-            second = pltpu.roll(block[:, LANES:], turn, 1)
-            cut = jnp.where(lane < LANES - shift, first, second)
-            cut = pltpu.roll(cut, PATCH + 8 - top % 8, 0)[:PATCH]
-            window[pl.ds(pl.multiple_of(i * PATCH, PATCH), PATCH), t * LANES : (t + 1) * LANES] = cut.astype(BF)
-        return carry
-
-    lax.fori_loop(0, rows, step, 0)
-
-
-def transform(block, along_ref, down_ref):
-    part = dot(block, along_ref[0]) + dot(block, along_ref[1])
-    high, low = split(part)
-    both = dot(down_ref[...], jnp.concatenate([high, low], 0))
+    deep = lax.broadcasted_iota(jnp.int32, (PATCH // 8, 8, LANES), 1)
+    for t in range(2):
+        j = 2 * c + t
+        top = OFFMAX + off_ref[s, 0, i, j]
+        ox = off_ref[s, 1, i, j]
+        left = (ox < 0).astype(jnp.int32)
+        base = pl.multiple_of((j + 1 - left) * LANES, LANES)
+        shift = ox + LANES * left
+        aligned = pl.multiple_of(i * PATCH + jnp.bitwise_and(top, -8), 8)
+        block = padded[pl.ds(aligned, PATCH + 8), pl.ds(base, 2 * LANES)]
+        turn = jnp.bitwise_and(LANES - shift, LANES - 1)
+        first = pltpu.roll(block[:, :LANES], turn, 1)
+        second = pltpu.roll(block[:, LANES:], turn, 1)
+        cut = jnp.where(lane < LANES - shift, first, second)
+        over = jnp.bitwise_and(top, 7)
+        cut = pltpu.roll(cut.reshape(PATCH // 8 + 1, 8, LANES), jnp.bitwise_and(8 - over, 7), 1)
+        cut = jnp.where(deep < 8 - over, cut[:-1], cut[1:]).reshape(PATCH, LANES)
+        window[i * PATCH : (i + 1) * PATCH, t * LANES : (t + 1) * LANES] = cut.astype(BF)
+
+
+def first_stage(block, along_ref, parts):
+    high, low = split(dot(jnp.concatenate([block, block], 1), along_ref[...]))
+    rows = parts.shape[0]
+    parts[:, :PATCH] = high.reshape(rows, PATCH, 2 * PATCH)
+    parts[:, PATCH:] = low.reshape(rows, PATCH, 2 * PATCH)
+
+
+def second_stage(part, down_ref):
+    both = dot(down_ref[...], part)
     return both[:PATCH] + both[PATCH:]
 
 
@@ -145,27 +147,32 @@
             out_ref[r : r + 8, q : q + LANES] = coef[r : r + 8, q : q + LANES] - mean
 
 
-def own_kernel(off_ref, image_ref, low_ref, high_ref, along_ref, down_ref, patch_out, window_out, padded, window):
+def patch_kernel(image_ref, along_ref, down_ref, out_ref, parts):
+    rows = image_ref.shape[0] // PATCH
+    s, c = pl.program_id(0), pl.program_id(1)
+    first_stage(image_ref[...], along_ref, parts)
+    for i in range(rows):
+        store_coefficients(out_ref.at[s, c, i], second_stage(parts[i], down_ref))
+
+
+def window_kernel(off_ref, image_ref, low_ref, high_ref, along_ref, down_ref, out_ref, padded, window, parts):
     s, c = pl.program_id(0), pl.program_id(1)
     rows = image_ref.shape[0] // PATCH
 
     @pl.when(c == 0)
     def _():
         fill_padded(padded, image_ref, low_ref, high_ref)
-
-    fill_windows(window, padded, off_ref, s, c, rows)
-    lanes = pl.ds(pl.multiple_of(c * 2 * LANES, 2 * LANES), 2 * LANES)
-
-    def step(i, carry):
-        down = pl.ds(pl.multiple_of(i * PATCH, PATCH), PATCH)
-        store_coefficients(patch_out.at[i], transform(image_ref[down, lanes], along_ref, down_ref))
-        store_coefficients(window_out.at[i], transform(window[down, :], along_ref, down_ref))
-        return carry
-
-    lax.fori_loop(0, rows, step, 0, unroll=2)
-
-
-def correlate(a_ref, b_ref, coef, pieces, rows_ref, cols_ref):
+        for i in range(rows):
+            fill_window_row(window.at[0], padded, off_ref, s, 0, i)
+
+    first_stage(window[c % 2], along_ref, parts)
+    following = jnp.minimum(c + 1, pl.num_programs(1) - 1)
+    for i in range(rows):
+        store_coefficients(out_ref.at[s, c, i], second_stage(parts[i], down_ref))
+        fill_window_row(window.at[(c + 1) % 2], padded, off_ref, s, following, i)
+
+
+def cross(a_ref, b_ref, coef, pieces):
     lane = lax.broadcasted_iota(jnp.int32, (16, LANES), 1)
     row = lax.broadcasted_iota(jnp.int32, (16, LANES), 0)
     sign_j = jnp.where(lane % HALF == 0, -1.0, 1.0).astype(F32)
@@ -195,9 +202,13 @@
             coef[where, lanes] = value
             pieces[where, lanes] = high
             pieces[slice(PATCH + where.start, PATCH + where.stop), lanes] = low
+    return jnp.sum(total, axis=0, keepdims=True)
+
+
+def moments(coef, pieces, rows_ref, cols_ref):
     down = dot(rows_ref[...], pieces[...])
+    across = dot(pieces[...], cols_ref[...])
     down = down[:HALF] + down[HALF:]
-    across = dot(pieces[...], cols_ref[...])
     across = across[:PATCH, :LANES] + across[:PATCH, LANES:] + across[PATCH:, :LANES]
     row8 = lax.broadcasted_iota(jnp.int32, (8, 2 * LANES), 0)
     head = down[0:8]
@@ -211,14 +222,13 @@
         piece = across[8 * g : 8 * g + 8]
         other = jnp.where(lane8, -float(HALF) * piece, coef[8 * g : 8 * g + 8, LANES:])
         moment_c = moment_c + other * piece
-    add = lambda x: jnp.sum(x, axis=0, keepdims=True)
-    return add(total), add(moment_r), add(moment_c)
+    return jnp.sum(moment_r, axis=0, keepdims=True), jnp.sum(moment_c, axis=0, keepdims=True)
 
 
 def pair_kernel(
     place_ref, off_ref, image_ref, low_ref, high_ref, along_ref, down_ref, rows_ref, cols_ref,
     own_patch, own_window, fwd_ref, bwd_ref, valid_ref, flow_out, tile_out,
-    padded, window, left, right, coef, pieces, sums,
+    padded, window, parts, left, right, coef, pieces, sums,
 ):
     s, c = pl.program_id(0), pl.program_id(1)
     rows = image_ref.shape[0] // PATCH
@@ -227,21 +237,38 @@
     @pl.when(c == 0)
     def _():
         fill_padded(padded, image_ref, low_ref, high_ref)
-
-    fill_windows(window, padded, off_ref, s, c, rows)
+        for i in range(rows):
+            fill_window_row(window.at[0], padded, off_ref, s, 0, i)
+
     lanes = pl.ds(pl.multiple_of(c * 2 * LANES, 2 * LANES), 2 * LANES)
-
-    def step(i, carry):
-        down = pl.ds(pl.multiple_of(i * PATCH, PATCH), PATCH)
-        store_coefficients(left, transform(image_ref[down, lanes], along_ref, down_ref))
-        store_coefficients(right, transform(window[down, :], along_ref, down_ref))
-        forward = correlate(own_patch.at[i], right, coef.at[0], pieces.at[0], rows_ref, cols_ref)
-        backward = correlate(left, own_window.at[i], coef.at[1], pieces.at[1], rows_ref, cols_ref)
-        for k, value in enumerate(forward + backward):
-            sums[k, c, pl.ds(i, 1), :] = value
-        return carry
-
-    lax.fori_loop(0, rows, step, 0)
+    first_stage(image_ref[:, lanes], along_ref, parts.at[0])
+    first_stage(window[c % 2], along_ref, parts.at[1])
+    following = jnp.minimum(c + 1, pairs - 1)
+
+    def spectra(i):
+        store_coefficients(left.at[i % 2], second_stage(parts[0, i], down_ref))
+        store_coefficients(right.at[i % 2], second_stage(parts[1, i], down_ref))
+
+    def products(i):
+        k = i % 2
+        sums[0, c, i : i + 1, :] = cross(own_patch.at[s, c, i], right.at[k], coef.at[0, k], pieces.at[0, k])
+        sums[3, c, i : i + 1, :] = cross(left.at[k], own_window.at[s, c, i], coef.at[1, k], pieces.at[1, k])
+
+    def centroid(i):
+        for d in range(2):
+            by_row, by_col = moments(coef.at[d, i % 2], pieces.at[d, i % 2], rows_ref, cols_ref)
+            sums[3 * d + 1, c, i : i + 1, :] = by_row
+            sums[3 * d + 2, c, i : i + 1, :] = by_col
+
+    spectra(0)
+    for i in range(rows):
+        if i + 1 < rows:
+            spectra(i + 1)
+        products(i)
+        fill_window_row(window.at[(c + 1) % 2], padded, off_ref, s, following, i)
+        if i:
+            centroid(i - 1)
+    centroid(rows - 1)
 
     @pl.when(c == pairs - 1)
     def _():
@@ -333,33 +360,46 @@
 SCALARS = pl.BlockSpec(memory_space=pltpu.SMEM)
 
 
-def body(image, fwd_offset, bwd_offset, valid):
+PARAMS = pltpu.CompilerParams(vmem_limit_bytes=24 * 1024 * 1024)
+
+
+def cost(flops):
+    return pl.CostEstimate(flops=flops, bytes_accessed=10**7, transcendentals=0)
+
+
+def coef_layout(sec_dev, rows, pairs):
+    return pltpu.VMEM((sec_dev, pairs, rows, PATCH, 2 * PATCH), F32), pl.BlockSpec(memory_space=pltpu.VMEM)
+
+
+def patch_spectra(image, rows, pairs):
     sec_dev, height, width = image.shape
-    rows, count = valid.shape[1:]
-    pairs = count // 2
-    sec_size, tile_size = lax.axis_size("sec"), lax.axis_size("tile")
-    sections = sec_dev * sec_size
-    along, down, form_rows, form_cols = (jnp.asarray(t) for t in tables())
-
-    earlier = [(i, i - 1) for i in range(1, sec_size)]
-    arriving = lax.ppermute(image[:1], "sec", earlier)
-    up = [(i, i + 1) for i in range(tile_size - 1)]
-    back = [(i + 1, i) for i in range(tile_size - 1)]
-    low = lax.ppermute(image[:, -OFFMAX:], "tile", up)
-    high = lax.ppermute(image[:, :OFFMAX], "tile", back)
-    edges = lax.ppermute(jnp.concatenate([low[:1], high[:1]], 1), "sec", earlier)
-    after = jnp.concatenate([image[1:], arriving], 0)
-    after_low = jnp.concatenate([low[1:], edges[:, :OFFMAX]], 0)
-    after_high = jnp.concatenate([high[1:], edges[:, OFFMAX:]], 0)
-
-    coef_shape = jax.ShapeDtypeStruct((sec_dev, pairs, rows, PATCH, 2 * PATCH), F32)
-    coef_spec = pl.BlockSpec((None, None, rows, PATCH, 2 * PATCH), lambda s, c: (s, c, 0, 0, 0))
-    padded = pltpu.VMEM((height + 2 * OFFMAX + 8, width + 2 * LANES), F32)
-    window = pltpu.VMEM((height, 2 * LANES), BF)
-    own_patch, own_window = pl.pallas_call(
-        own_kernel,
+    along, down, _, _ = (jnp.asarray(t) for t in tables())
+    shape, spec = coef_layout(sec_dev, rows, pairs)
+    return pl.pallas_call(
+        patch_kernel,
         grid=(sec_dev, pairs),
-        out_shape=(coef_shape, coef_shape),
+        out_shape=shape,
+        in_specs=[
+            pl.BlockSpec((None, height, 2 * LANES), lambda s, c: (s, 0, c)),
+            whole_spec(along.shape),
+            whole_spec(down.shape),
+        ],
+        out_specs=spec,
+        scratch_shapes=[pltpu.VMEM((rows, 2 * PATCH, 2 * PATCH), BF)],
+        compiler_params=PARAMS,
+        cost_estimate=cost(5 * 10**9),
+        name="patch_spectra",
+    )(image, along, down)
+
+
+def window_spectra(offset, image, low, high, rows, pairs):
+    sec_dev, height, width = image.shape
+    along, down, _, _ = (jnp.asarray(t) for t in tables())
+    shape, spec = coef_layout(sec_dev, rows, pairs)
+    return pl.pallas_call(
+        window_kernel,
+        grid=(sec_dev, pairs),
+        out_shape=shape,
         in_specs=[
             SCALARS,
             section_spec(image.shape),
@@ -368,17 +408,26 @@
             whole_spec(along.shape),
             whole_spec(down.shape),
         ],
-        out_specs=(coef_spec, coef_spec),
-        scratch_shapes=[padded, window],
-        compiler_params=pltpu.CompilerParams(vmem_limit_bytes=48 * 1024 * 1024),
-        cost_estimate=pl.CostEstimate(flops=10**10, bytes_accessed=10**7, transcendentals=0),
-        name="own_spectra",
-    )(bwd_offset, image, low, high, along, down)
-
-    place = lax.axis_index("sec") * sec_dev
-    notlast = (place + jnp.arange(sec_dev, dtype=jnp.int32) < sections - 1).astype(jnp.int32)
+        out_specs=spec,
+        scratch_shapes=[
+            pltpu.VMEM((height + 2 * OFFMAX + 8, width + 2 * LANES), F32),
+            pltpu.VMEM((2, height, 2 * LANES), BF),
+            pltpu.VMEM((rows, 2 * PATCH, 2 * PATCH), BF),
+        ],
+        compiler_params=PARAMS,
+        cost_estimate=cost(5 * 10**9),
+        name="window_spectra",
+    )(offset, image, low, high, along, down)
+
+
+def pair_flows(notlast, fwd_offset, after, after_low, after_high, own_patch, own_window, bwd_offset, valid):
+    sec_dev, height, width = after.shape
+    rows, count = valid.shape[1:]
+    pairs = count // 2
+    along, down, form_rows, form_cols = (jnp.asarray(t) for t in tables())
+    _, coef_spec = coef_layout(sec_dev, rows, pairs)
     flow_shape = jax.ShapeDtypeStruct((sec_dev, 2, rows, count), F32)
-    pair_flow, tile = pl.pallas_call(
+    return pl.pallas_call(
         pair_kernel,
         grid=(sec_dev, pairs),
         out_shape=(flow_shape, jax.ShapeDtypeStruct((sec_dev, rows, LANES), F32)),
@@ -400,20 +449,46 @@
         ],
         out_specs=(section_spec(flow_shape.shape), section_spec((sec_dev, rows, LANES))),
         scratch_shapes=[
-            padded,
-            window,
-            pltpu.VMEM((PATCH, 2 * PATCH), F32),
-            pltpu.VMEM((PATCH, 2 * PATCH), F32),
+            pltpu.VMEM((height + 2 * OFFMAX + 8, width + 2 * LANES), F32),
+            pltpu.VMEM((2, height, 2 * LANES), BF),
+            pltpu.VMEM((2, rows, 2 * PATCH, 2 * PATCH), BF),
             pltpu.VMEM((2, PATCH, 2 * PATCH), F32),
-            pltpu.VMEM((2, 2 * PATCH, 2 * PATCH), BF),
+            pltpu.VMEM((2, PATCH, 2 * PATCH), F32),
+            pltpu.VMEM((2, 2, PATCH, 2 * PATCH), F32),
+            pltpu.VMEM((2, 2, 2 * PATCH, 2 * PATCH), BF),
             pltpu.VMEM((6, pairs, rows, LANES), F32),
         ],
-        compiler_params=pltpu.CompilerParams(vmem_limit_bytes=48 * 1024 * 1024),
-        cost_estimate=pl.CostEstimate(flops=10**10, bytes_accessed=10**7, transcendentals=0),
+        compiler_params=PARAMS,
+        cost_estimate=cost(2 * 10**10),
         name="pair_flows",
     )(notlast, fwd_offset, after, after_low, after_high, along, down, form_rows, form_cols,
       own_patch, own_window, fwd_offset, bwd_offset, valid)
 
+
+def body(image, fwd_offset, bwd_offset, valid):
+    sec_dev, height, width = image.shape
+    rows, count = valid.shape[1:]
+    pairs = count // 2
+    sec_size, tile_size = lax.axis_size("sec"), lax.axis_size("tile")
+    sections = sec_dev * sec_size
+    earlier = [(i, i - 1) for i in range(1, sec_size)]
+    arriving = lax.ppermute(image[:1], "sec", earlier)
+    up = [(i, i + 1) for i in range(tile_size - 1)]
+    back = [(i + 1, i) for i in range(tile_size - 1)]
+    low = lax.ppermute(image[:, -OFFMAX:], "tile", up)
+    high = lax.ppermute(image[:, :OFFMAX], "tile", back)
+    edges = lax.ppermute(jnp.concatenate([low[:1], high[:1]], 1), "sec", earlier)
+    after = jnp.concatenate([image[1:], arriving], 0)
+    after_low = jnp.concatenate([low[1:], edges[:, :OFFMAX]], 0)
+    after_high = jnp.concatenate([high[1:], edges[:, OFFMAX:]], 0)
+
+    own_patch = patch_spectra(image, rows, pairs)
+    own_window = window_spectra(bwd_offset, image, low, high, rows, pairs)
+    place = lax.axis_index("sec") * sec_dev
+    notlast = (place + jnp.arange(sec_dev, dtype=jnp.int32) < sections - 1).astype(jnp.int32)
+    pair_flow, tile = pair_flows(
+        notlast, fwd_offset, after, after_low, after_high, own_patch, own_window, bwd_offset, valid
+    )
     devices = sec_size * tile_size
     everywhere = lax.all_to_all(jnp.broadcast_to(tile[None], (devices,) + tile.shape), ("sec", "tile"), 0, 0)
     everywhere = (
@@ -424,10 +499,11 @@
     where = jnp.stack([place, lax.axis_index("tile") * rows]).astype(jnp.int32)
     mesh_shift = pl.pallas_call(
         mesh_kernel,
-        out_shape=flow_shape,
+        out_shape=jax.ShapeDtypeStruct(pair_flow.shape, F32),
         in_specs=[SCALARS, pl.BlockSpec(memory_space=pltpu.VMEM)],
         out_specs=pl.BlockSpec(memory_space=pltpu.VMEM),
         scratch_shapes=[pltpu.VMEM((sections, tile_size * rows, LANES), F32)],
+        compiler_params=pltpu.CompilerParams(vmem_limit_bytes=8 * 1024 * 1024),
         name="relax",
     )(where, everywhere)
     return pair_flow, mesh_shift

time: 88 us -> 61.9 us (0.70)
  Pallas kernels: 52.6 us -> 27.9 us
  waiting for transfers between devices: 12.5 us -> 8.33 us
  starting transfers between devices: 14.8 us -> 17.5 us
    pallas_call x3 -> x4, Pallas kernels: 52.6 us -> 27.9 us  [the longest x1 15.1 us: pair_flows(): pl.pallas_call(pair_kernel, grid=(sec_dev, pairs), out_shape=(flow_shape,...]
    ppermute x1, waiting for transfers between devices: 4.43 us -> 0.01 us  [body(): high = lax.ppermute(image[:, :OFFMAX], 'tile', back)]
    all_to_all x1, starting transfers between devices: 6 us -> 8.45 us  [body(): lax.all_to_all(jnp.broadcast_to(tile[None], (devices,) + tile.shape), ('s...]
    unnamed x18 -> x26, local copies, waits for them, and re-layouts: 4.82 us -> 5.42 us
  transfers between devices with their start and end apart: 5 -> 5, of which waited for: 3 -> 1; matrix products, arithmetic and copies ran while one was open for 2% -> 1% of each run, Pallas kernels for 20% -> 18%
where the time goes in v2:
time: 61.9 us; the launch traced here: 61.5 us
  Pallas kernels  27.9 us (45%)
  starting transfers between devices  17.5 us (28%)
  waiting for transfers between devices  8.33 us (13%)
  local copies, waits for them, and re-layouts  6.86 us (11%)
  between operations  0.85 us (1%)
    pallas_call x1, Pallas kernels, pair_flows(): pl.pallas_call(pair_kernel, grid=(sec_dev, pairs), out_shape=(flow_shape,...  15.1 us
    all_to_all x1, starting transfers between devices, body(): lax.all_to_all(jnp.broadcast_to(tile[None], (devices,) + tile.shape), ('s...  8.45 us
    all_to_all x1, waiting for transfers between devices, body(): lax.all_to_all(jnp.broadcast_to(tile[None], (devices,) + tile.shape), ('s...  8.32 us
    pallas_call x1, Pallas kernels, window_spectra(): pl.pallas_call(window_kernel, grid=(sec_dev, pairs), out_shape=shape, in_...  6.26 us
    unnamed x26, local copies, waits for them, and re-layouts  5.42 us
    ppermute x1, starting transfers between devices, body(): low = lax.ppermute(image[:, -OFFMAX:], 'tile', up)  4.92 us
    pallas_call x1, Pallas kernels, patch_spectra(): pl.pallas_call(patch_kernel, grid=(sec_dev, pairs), out_shape=shape, in_s...  4.86 us
    pallas_call x1, Pallas kernels, body(): pl.pallas_call(mesh_kernel, out_shape=jax.ShapeDtypeStruct(pair_flow.shap...  1.67 us
  transfers between devices with their start and end apart: 5, of which 1 were waited for; matrix products, arithmetic and copies ran while one was open for 1% of the time, Pallas kernels for 18%

profile of v2, /device:TPU:0, one launch (start us, length us, event | category | flops | bytes accessed | tf_op | source)
XLA Modules:
  0.0 61.5 jit_solution(11851060397329918883)
XLA Ops:
  0.6 1.3 %collective-permute-start = (bf16[1,1024,1024]{2,1,0:T(8,128)(2,1)}, bf16[1,1024,1024]{2,1,0:T(8,128)(2,1)}, u32[]{:S(2)}, u32[]{:S(2)}) collective-permute-start(bf16[1,1024,1024]{2,1,0:T(8,128)(2,1)} %image_ref.3), channel_id=1, source_target_pairs={{4,0},{8,4},{12,8},{16,12},{20,16},{24,20},{28,24},{5,1},{9,5},{13... | collective-permute-start | bytes 6291464 | tf_op jit(solution)/shard_map/ppermute | solution.py:475
  1.9 0.8 %fusion = (bf16[1,16,1024]{2,1,0:T(8,128)(2,1)S(1)}, bf16[1,16,1024]{2,1,0:T(8,128)(2,1)S(1)}) fusion(bf16[1,1024,1024]{2,1,0:T(8,128)(2,1)} %image_ref.3), kind=kLoop, calls=%fused_computation.2 | loop fusion | bytes 131072 | tf_op jit(solution)/shard_map/slice | solution.py:478
  2.7 4.9 %collective-permute-start.1 = (bf16[1,16,1024]{2,1,0:T(8,128)(2,1)S(1)}, bf16[1,16,1024]{2,1,0:T(8,128)(2,1)S(1)}, u32[]{:S(2)}, u32[]{:S(2)}) collective-permute-start(bf16[1,16,1024]{2,1,0:T(8,128)(2,1)S(1)} %get-tuple-element.6), channel_id=1, source_target_pairs={{0,1},{1,2},{2,3},{4,5},{5,6},{6,7},{8,9},{9,10},{10,11},{12,13},{... | collective-permute-start | bytes 98312 | tf_op jit(solution)/shard_map/ppermute | solution.py:478
  7.6 1.3 %collective-permute-start.2 = (bf16[1,16,1024]{2,1,0:T(8,128)(2,1)S(1)}, bf16[1,16,1024]{2,1,0:T(8,128)(2,1)S(1)}, u32[]{:S(2)}, u32[]{:S(2)}) collective-permute-start(bf16[1,16,1024]{2,1,0:T(8,128)(2,1)S(1)} %get-tuple-element.7), channel_id=1, source_target_pairs={{1,0},{2,1},{3,2},{5,4},{6,5},{7,6},{9,8},{10,9},{11,10},{13,12},{... | collective-permute-start | bytes 98312 | tf_op jit(solution)/shard_map/ppermute | solution.py:479
  8.9 0.0 copy-start
  8.9 1.6 %copy-done = bf16[1,1024,1024]{2,1,0:T(8,128)(2,1)S(1)} copy-done((bf16[1,1024,1024]{2,1,0:T(8,128)(2,1)S(1)}, bf16[1,1024,1024]{2,1,0:T(8,128)(2,1)}, u32[]{:S(2)}) %copy-start) | copy-done | bytes 2097176
  10.5 0.9 %copy-done.5 = bf16[512,256]{1,0:T(8,128)(2,1)S(1)} copy-done((bf16[512,256]{1,0:T(8,128)(2,1)S(1)}, bf16[512,256]{1,0:T(8,128)(2,1)}, u32[]{:S(2)}) %copy-start.5) | copy-done | bytes 262168
  11.5 0.9 %copy-done.7 = bf16[256,256]{1,0:T(8,128)(2,1)S(1)} copy-done((bf16[256,256]{1,0:T(8,128)(2,1)S(1)}, bf16[256,256]{1,0:T(8,128)(2,1)}, u32[]{:S(2)}) %copy-start.7) | copy-done | bytes 131096
  12.4 4.9 %patch_spectra.1.own_patch = f32[1,4,8,128,256]{4,3,2,1,0:T(8,128)S(1)} custom-call(bf16[1,1024,1024]{2,1,0:T(8,128)(2,1)S(1)} %copy-done, bf16[512,256]{1,0:T(8,128)(2,1)S(1)} %copy-done.5, bf16[256,256]{1,0:T(8,128)(2,1)S(1)} %copy-done.7), custom_call_target="tpu_custom_call" | custom-call | flops 5000000000 | bytes 10000000 | tf_op jit(solution)/shard_map/patch_spectra/pallas_call | solution.py:378
  17.3 0.0 copy-start.11
  17.3 1.9 %copy-done.11 = f32[1,4,8,128,256]{4,3,2,1,0:T(8,128)} copy-done((f32[1,4,8,128,256]{4,3,2,1,0:T(8,128)}, f32[1,4,8,128,256]{4,3,2,1,0:T(8,128)S(1)}, u32[]{:S(2)}) %copy-start.11) | copy-done | bytes 4194328
  19.2 0.0 collective-permute-done.1.low_ref
  19.2 0.0 collective-permute-done.2.high_ref
  19.2 0.0 copy-start.2
  19.2 0.0 copy-start.4
  19.3 0.0 copy-start.9
  19.3 0.0 copy-start.10
  19.3 0.0 copy-start.12
  19.3 1.6 %collective-permute-start.3 = (bf16[1,32,1024]{2,1,0:T(8,128)(2,1)S(1)}, bf16[1,32,1024]{2,1,0:T(8,128)(2,1)S(1)}, u32[]{:S(2)}, u32[]{:S(2)}) collective-permute-start(bf16[1,32,1024]{2,1,0:T(8,128)(2,1)S(1)} %pad_maximum_fusion), channel_id=1, source_target_pairs={{4,0},{8,4},{12,8},{16,12},{20,16},{24,20},{28,24},{5,1},{9,5},{13... | collective-permute-start | bytes 196616 | tf_op jit(solution)/shard_map/ppermute | solution.py:480
  20.9 6.3 %window_spectra.1.own_window = f32[1,4,8,128,256]{4,3,2,1,0:T(8,128)S(1)} custom-call(s32[1,2,8,8]{3,2,1,0:T(8,128)S(1)} %copy-done.3, bf16[1,1024,1024]{2,1,0:T(8,128)(2,1)S(1)} %copy-done.1, bf16[1,16,1024]{2,1,0:T(8,128)(2,1)S(1)} %collective-permute-done.1.low_ref, bf16[1,16,1024]{2,1,0:T(8,128)(2,1)S(1)} %collective-permute-done.2.high_ref, ...), custom_call_target="tpu_custom_call" | custom-call | flops 5000000000 | bytes 10000000 | tf_op jit(solution)/shard_map/window_spectra/pallas_call | solution.py:399
  27.2 0.0 collective-permute-done.3
  27.2 0.0 collective-permute-done.image_ref
  27.2 0.0 copy-done.2
  27.2 0.0 copy-done.4
  27.2 0.0 copy-done.9
  27.2 0.0 copy-done.10
  27.2 15.1 %pair_flows.1 = (f32[1,2,8,8]{3,2,1,0:T(8,128)}, f32[1,8,128]{2,1,0:T(8,128)S(1)}) custom-call(s32[1]{0:T(128)S(6)} %convert_element_type.3.place_ref, s32[1,2,8,8]{3,2,1,0:T(8,128)S(1)} %copy-done.2, bf16[1,1024,1024]{2,1,0:T(8,128)(2,1)} %collective-permute-done.image_ref, bf16[1,16,1024]{2,1,0:T(8,128)(2,1)S(1)} %get-tuple-element.9.low_ref, ...), custom_call_target="tpu_custom_call" | custom-call | flops 20000000000 | bytes 10000000 | tf_op jit(solution)/shard_map/pair_flows/pallas_call | solution.py:430
  42.4 0.7 %broadcast_in_dim.9 = f32[32,1,8,128]{3,2,1,0:T(8,128)} broadcast(f32[8,128]{1,0:T(8,128)S(1)} %bitcast.5), dimensions={2,3} | broadcast | bytes 135168 | tf_op jit(solution)/shard_map/broadcast_in_dim | solution.py:493
  43.0 8.4 %all-to-all-start = ((f32[32,1,8,128]{3,2,1,0:T(8,128)}), f32[32,1,8,128]{3,2,1,0:T(8,128)S(1)}, u32[]{:S(2)}, u32[]{:S(2)}) async-start(f32[32,1,8,128]{3,2,1,0:T(8,128)} %broadcast_in_dim.9), calls=%async_computation | async-start | bytes 262144 | tf_op jit(solution)/shard_map/all_to_all | solution.py:493
  51.5 0.1 pad_add_fusion.place_ref
  51.5 8.3 %all-to-all-done = f32[32,1,8,128]{3,2,1,0:T(8,128)S(1)} async-done(((f32[32,1,8,128]{3,2,1,0:T(8,128)}), f32[32,1,8,128]{3,2,1,0:T(8,128)S(1)}, u32[]{:S(2)}, u32[]{:S(2)}) %all-to-all-start) | async-done | bytes 131104 | tf_op jit(solution)/shard_map/all_to_all | solution.py:493
  59.9 1.7 %relax.1 = f32[1,2,8,8]{3,2,1,0:T(8,128)} custom-call(s32[2]{0:T(128)S(1)} %pad_add_fusion.place_ref, f32[8,32,128]{2,1,0:T(8,128)S(1)} %bitcast.4), custom_call_target="tpu_custom_call" | custom-call | tf_op jit(solution)/shard_map/relax/pallas_call | solution.py:500
  (13 shorter events, 0.0 us)
Async XLA Ops:
  0.6 26.6 %collective-permute-start = (bf16[1,1024,1024]{2,1,0:T(8,128)(2,1)}, bf16[1,1024,1024]{2,1,0:T(8,128)(2,1)}, u32[]{:S(2)}, u32[]{:S(2)}) collective-permute-start(bf16[1,1024,1024]{2,1,0:T(8,128)(2,1)} %image_ref.3), channel_id=1, source_target_pairs={{4,0},{8,4},{12,8},{16,12},{20,16},{24,20},{28,24},{5,1},{9,5},{13... | collective-permute-start | bytes 6291464 | tf_op jit(solution)/shard_map/ppermute | solution.py:475
  2.7 16.5 %collective-permute-start.1 = (bf16[1,16,1024]{2,1,0:T(8,128)(2,1)S(1)}, bf16[1,16,1024]{2,1,0:T(8,128)(2,1)S(1)}, u32[]{:S(2)}, u32[]{:S(2)}) collective-permute-start(bf16[1,16,1024]{2,1,0:T(8,128)(2,1)S(1)} %get-tuple-element.6), channel_id=1, source_target_pairs={{0,1},{1,2},{2,3},{4,5},{5,6},{6,7},{8,9},{9,10},{10,11},{12,13},{... | collective-permute-start | bytes 98312 | tf_op jit(solution)/shard_map/ppermute | solution.py:478
  7.6 11.6 %collective-permute-start.2 = (bf16[1,16,1024]{2,1,0:T(8,128)(2,1)S(1)}, bf16[1,16,1024]{2,1,0:T(8,128)(2,1)S(1)}, u32[]{:S(2)}, u32[]{:S(2)}) collective-permute-start(bf16[1,16,1024]{2,1,0:T(8,128)(2,1)S(1)} %get-tuple-element.7), channel_id=1, source_target_pairs={{1,0},{2,1},{3,2},{5,4},{6,5},{7,6},{9,8},{10,9},{11,10},{13,12},{... | collective-permute-start | bytes 98312 | tf_op jit(solution)/shard_map/ppermute | solution.py:479
  8.9 1.6 %copy-start = (bf16[1,1024,1024]{2,1,0:T(8,128)(2,1)S(1)}, bf16[1,1024,1024]{2,1,0:T(8,128)(2,1)}, u32[]{:S(2)}) copy-start(bf16[1,1024,1024]{2,1,0:T(8,128)(2,1)} %image_ref.3) | copy-start | bytes 6291460
  10.5 0.9 %copy-start.5 = (bf16[512,256]{1,0:T(8,128)(2,1)S(1)}, bf16[512,256]{1,0:T(8,128)(2,1)}, u32[]{:S(2)}) copy-start(bf16[512,256]{1,0:T(8,128)(2,1)} %constant.21.clone.along_ref) | copy-start | bytes 786436
  11.5 0.9 %copy-start.7 = (bf16[256,256]{1,0:T(8,128)(2,1)S(1)}, bf16[256,256]{1,0:T(8,128)(2,1)}, u32[]{:S(2)}) copy-start(bf16[256,256]{1,0:T(8,128)(2,1)} %constant.22.clone.down_ref) | copy-start | bytes 393220
  12.4 8.5 %copy-start.1 = (bf16[1,1024,1024]{2,1,0:T(8,128)(2,1)S(1)}, bf16[1,1024,1024]{2,1,0:T(8,128)(2,1)}, u32[]{:S(2)}) copy-start(bf16[1,1024,1024]{2,1,0:T(8,128)(2,1)} %image_ref.3) | copy-start | bytes 6291460
  12.4 8.5 %copy-start.3 = (s32[1,2,8,8]{3,2,1,0:T(8,128)S(1)}, s32[1,2,8,8]{3,2,1,0:T(8,128)}, u32[]{:S(2)}) copy-start(s32[1,2,8,8]{3,2,1,0:T(8,128)} %bwd_ref.1) | copy-start | bytes 1540
  12.4 8.5 %copy-start.6 = (bf16[512,256]{1,0:T(8,128)(2,1)S(1)}, bf16[512,256]{1,0:T(8,128)(2,1)}, u32[]{:S(2)}) copy-start(bf16[512,256]{1,0:T(8,128)(2,1)} %constant.21.clone.along_ref) | copy-start | bytes 786436
  12.4 8.5 %copy-start.8 = (bf16[256,256]{1,0:T(8,128)(2,1)S(1)}, bf16[256,256]{1,0:T(8,128)(2,1)}, u32[]{:S(2)}) copy-start(bf16[256,256]{1,0:T(8,128)(2,1)} %constant.22.clone.down_ref) | copy-start | bytes 393220
  17.3 1.9 %copy-start.11 = (f32[1,4,8,128,256]{4,3,2,1,0:T(8,128)}, f32[1,4,8,128,256]{4,3,2,1,0:T(8,128)S(1)}, u32[]{:S(2)}) copy-start(f32[1,4,8,128,256]{4,3,2,1,0:T(8,128)S(1)} %patch_spectra.1.own_patch) | copy-start | bytes 12582916
  19.2 8.0 %copy-start.2 = (s32[1,2,8,8]{3,2,1,0:T(8,128)S(1)}, s32[1,2,8,8]{3,2,1,0:T(8,128)}, u32[]{:S(2)}) copy-start(s32[1,2,8,8]{3,2,1,0:T(8,128)} %fwd_ref.1) | copy-start | bytes 1540
  19.2 8.0 %copy-start.4 = (s32[1,8,8]{2,1,0:T(8,128)S(1)}, s32[1,8,8]{2,1,0:T(8,128)}, u32[]{:S(2)}) copy-start(s32[1,8,8]{2,1,0:T(8,128)} %valid_ref.1) | copy-start | bytes 772
  19.3 8.0 %copy-start.9 = (bf16[256,256]{1,0:T(8,128)(2,1)S(1)}, bf16[256,256]{1,0:T(8,128)(2,1)}, u32[]{:S(2)}) copy-start(bf16[256,256]{1,0:T(8,128)(2,1)} %constant.24.clone.cols_ref) | copy-start | bytes 393220
  19.3 8.0 %copy-start.10 = (bf16[128,256]{1,0:T(8,128)(2,1)S(1)}, bf16[128,256]{1,0:T(8,128)(2,1)}, u32[]{:S(2)}) copy-start(bf16[128,256]{1,0:T(8,128)(2,1)} %constant.23.clone.rows_ref) | copy-start | bytes 196612
  19.3 8.0 %copy-start.12 = (f32[1,4,8,128,256]{4,3,2,1,0:T(8,128)S(1)}, f32[1,4,8,128,256]{4,3,2,1,0:T(8,128)}, u32[]{:S(2)}) copy-start(f32[1,4,8,128,256]{4,3,2,1,0:T(8,128)} %copy-done.11) | copy-start | bytes 12582916
  19.3 7.9 %collective-permute-start.3 = (bf16[1,32,1024]{2,1,0:T(8,128)(2,1)S(1)}, bf16[1,32,1024]{2,1,0:T(8,128)(2,1)S(1)}, u32[]{:S(2)}, u32[]{:S(2)}) collective-permute-start(bf16[1,32,1024]{2,1,0:T(8,128)(2,1)S(1)} %pad_maximum_fusion), channel_id=1, source_target_pairs={{4,0},{8,4},{12,8},{16,12},{20,16},{24,20},{28,24},{5,1},{9,5},{13... | collective-permute-start | bytes 196616 | tf_op jit(solution)/shard_map/ppermute | solution.py:480
  43.0 16.9 %all-to-all-start = ((f32[32,1,8,128]{3,2,1,0:T(8,128)}), f32[32,1,8,128]{3,2,1,0:T(8,128)S(1)}, u32[]{:S(2)}, u32[]{:S(2)}) async-start(f32[32,1,8,128]{3,2,1,0:T(8,128)} %broadcast_in_dim.9), calls=%async_computation | async-start | bytes 262144 | tf_op jit(solution)/shard_map/all_to_all | solution.py:493

commit v3 on v2

--- a/solution.py
+++ b/solution.py
@@ -298,55 +298,83 @@
             flow_out[comp] = flow
             flows.append(flow)
         fill = jnp.zeros((rows, LANES - 4 * count), F32)
-        tile_out[...] = jnp.concatenate(flows + [weight, weight, fill], axis=1)
-
-
-def mesh_kernel(place_ref, all_ref, shift_out, held):
-    sections, height, _ = all_ref.shape
+        wide = jnp.concatenate(flows + [weight, weight, fill], axis=1)
+        row = lax.broadcasted_iota(jnp.int32, (rows, LANES), 0)
+        group = 2 * count
+        packed = []
+        for begin in (0, group):
+            line = jnp.zeros((rows, LANES), F32)
+            for i in range(rows):
+                turned = pltpu.roll(wide, (group * i - begin) % LANES, 1)
+                line = jnp.where(jnp.logical_and(row == i, lane // group == i), turned, line)
+            packed.append(jnp.sum(line, axis=0, keepdims=True))
+        packed = jnp.concatenate(packed, axis=0)
+        for k in range(tile_out.shape[0]):
+            tile_out[k, s] = packed
+
+
+def mesh_kernel(tiles, place_ref, all_ref, shift_out):
+    bands = all_ref.shape[0]
     sec_dev, _, rows, count = shift_out.shape
-    lane = lax.broadcasted_iota(jnp.int32, (1, height, LANES), 2)
-    down = lax.broadcasted_iota(jnp.int32, (1, height, LANES), 1)
-    used = lane < 2 * count
-    first = lane < count
+    group = 2 * count
+    assert rows * group == LANES
     everything = all_ref[...]
-    flow = jnp.where(used, everything, 0.0)
-    weight = jnp.where(used, pltpu.roll(everything, LANES - 2 * count, 2), 0.0)
+    flow, weight = everything[:, 0], everything[:, 1]
+    line = lax.broadcasted_iota(jnp.int32, (bands, LANES), 0)
+    lane = lax.broadcasted_iota(jnp.int32, (bands, LANES), 1)
+    band = line % tiles
+    col, is_x, patch_row = lane % count, lane // count % 2, lane // group
     pulled = weight * flow
-    counts = jnp.sum(jnp.sum(jnp.where(first, weight, 0.0), axis=1, keepdims=True), axis=2, keepdims=True)
-    weighted = jnp.sum(pulled, axis=1, keepdims=True)
-    lane1 = lax.broadcasted_iota(jnp.int32, (1, 1, LANES), 2)
-    sum_y = jnp.sum(jnp.where(lane1 < count, weighted, 0.0), axis=2, keepdims=True)
-    sum_x = jnp.sum(jnp.where(lane1 >= count, weighted, 0.0), axis=2, keepdims=True)
-    many = jnp.maximum(counts, 1.0)
-    mean = jnp.where(first, sum_y / many, sum_x / many)
-    starts = []
-    start = jnp.zeros((1, height, LANES), F32)
-    for k in range(sections):
-        starts.append(start)
-        start = start + mean[k : k + 1]
-    shift = jnp.concatenate(starts, 0)
-    zero = jnp.zeros((1, height, LANES), F32)
-    col = lane % count
-    has_left, has_right = (col > 0).astype(F32), (col < count - 1).astype(F32)
-    has_up, has_down = (down > 0).astype(F32), (down < height - 1).astype(F32)
+
+    def over_section(x):
+        total = x
+        for k in range(1, tiles):
+            total = total + jnp.where(band >= k, pltpu.roll(x, k, 0), pltpu.roll(x, bands - tiles + k, 0))
+        return total
+
+    sum_y = jnp.sum(jnp.where(is_x == 0, pulled, 0.0), axis=1, keepdims=True)
+    sum_x = jnp.sum(jnp.where(is_x == 1, pulled, 0.0), axis=1, keepdims=True)
+    counts = jnp.sum(jnp.where(is_x == 0, weight, 0.0), axis=1, keepdims=True)
+    sums = over_section(jnp.where(is_x == 0, sum_y, sum_x))
+    mean = sums / jnp.maximum(over_section(jnp.broadcast_to(counts, sums.shape)), 1.0)
+    shift = jnp.where(line >= tiles, pltpu.roll(mean, tiles, 0), 0.0)
+    reach = tiles
+    while reach < bands:
+        shift = shift + jnp.where(line >= reach, pltpu.roll(shift, reach, 0), 0.0)
+        reach *= 2
+    at_top, at_bottom = patch_row == 0, patch_row == rows - 1
+    one = lambda condition: condition.astype(F32)
+    has_left, has_right = one(col > 0), one(col < count - 1)
+    has_up = one(jnp.logical_or(band > 0, patch_row > 0))
+    has_down = one(jnp.logical_or(band < tiles - 1, patch_row < rows - 1))
     degree = has_left + has_right + has_up + has_down
+    not_first = one(line >= tiles)
+    not_end = one(line < bands - tiles)
+    weight_next, pulled_next = weight * not_end, pulled
     for _ in range(ITERS):
+        lower, upper = pltpu.roll(shift, group, 1), pltpu.roll(shift, LANES - group, 1)
+        above = jnp.where(at_top, pltpu.roll(lower, 1, 0), lower)
+        below = jnp.where(at_bottom, pltpu.roll(upper, bands - 1, 0), upper)
         plane = (
-            has_up * pltpu.roll(shift, 1, 1)
-            + has_down * pltpu.roll(shift, height - 1, 1)
-            + has_left * pltpu.roll(shift, 1, 2)
-            + has_right * pltpu.roll(shift, LANES - 1, 2)
+            has_up * above
+            + has_down * below
+            + has_left * pltpu.roll(shift, 1, 1)
+            + has_right * pltpu.roll(shift, LANES - 1, 1)
             - degree * shift
         )
-        after = jnp.concatenate([shift[1:], zero], 0)
-        spring = weight * (after - shift) - pulled
-        between = spring - jnp.concatenate([zero, spring[:-1]], 0)
+        spring = weight_next * (pltpu.roll(shift, bands - tiles, 0) - shift) - pulled_next
+        between = spring - not_first * pltpu.roll(spring, tiles, 0)
         shift = shift + 0.25 * (plane + between)
-    held[...] = shift
+    mine_line = lax.broadcasted_iota(jnp.int32, (bands, LANES), 0)
+    row = lax.broadcasted_iota(jnp.int32, (rows, LANES), 0)
     for k in range(sec_dev):
-        mine = held[place_ref[0] + k, pl.ds(pl.multiple_of(place_ref[1], 8), rows), :]
-        shift_out[k, 0] = mine[:, :count]
-        shift_out[k, 1] = mine[:, count : 2 * count]
+        mine = jnp.sum(jnp.where(mine_line == place_ref[0] + k * tiles, shift, 0.0), axis=0, keepdims=True)
+        spread = jnp.zeros((rows, LANES), F32)
+        wide = jnp.broadcast_to(mine, (rows, LANES))
+        for i in range(rows):
+            spread = jnp.where(row == i, pltpu.roll(wide, (LANES - group * i) % LANES, 1), spread)
+        shift_out[k, 0] = spread[:, :count]
+        shift_out[k, 1] = spread[:, count:group]
 
 
 def section_spec(shape):
@@ -361,6 +389,10 @@
 
 
 PARAMS = pltpu.CompilerParams(vmem_limit_bytes=24 * 1024 * 1024)
+
+
+def in_hbm(array):
+    return pltpu.with_memory_space_constraint(array, pltpu.HBM)
 
 
 def cost(flops):
@@ -389,7 +421,7 @@
         compiler_params=PARAMS,
         cost_estimate=cost(5 * 10**9),
         name="patch_spectra",
-    )(image, along, down)
+    )(*(in_hbm(x) for x in (image, along, down)))
 
 
 def window_spectra(offset, image, low, high, rows, pairs):
@@ -420,7 +452,7 @@
     )(offset, image, low, high, along, down)
 
 
-def pair_flows(notlast, fwd_offset, after, after_low, after_high, own_patch, own_window, bwd_offset, valid):
+def pair_flows(devices, notlast, fwd_offset, after, after_low, after_high, own_patch, own_window, bwd_offset, valid):
     sec_dev, height, width = after.shape
     rows, count = valid.shape[1:]
     pairs = count // 2
@@ -430,7 +462,7 @@
     return pl.pallas_call(
         pair_kernel,
         grid=(sec_dev, pairs),
-        out_shape=(flow_shape, jax.ShapeDtypeStruct((sec_dev, rows, LANES), F32)),
+        out_shape=(flow_shape, jax.ShapeDtypeStruct((devices, sec_dev, 2, LANES), F32)),
         in_specs=[
             SCALARS,
             SCALARS,
@@ -447,7 +479,7 @@
             section_spec(bwd_offset.shape),
             section_spec(valid.shape),
         ],
-        out_specs=(section_spec(flow_shape.shape), section_spec((sec_dev, rows, LANES))),
+        out_specs=(section_spec(flow_shape.shape), pl.BlockSpec(memory_space=pltpu.VMEM)),
         scratch_shapes=[
             pltpu.VMEM((height + 2 * OFFMAX + 8, width + 2 * LANES), F32),
             pltpu.VMEM((2, height, 2 * LANES), BF),
@@ -486,23 +518,21 @@
     own_window = window_spectra(bwd_offset, image, low, high, rows, pairs)
     place = lax.axis_index("sec") * sec_dev
     notlast = (place + jnp.arange(sec_dev, dtype=jnp.int32) < sections - 1).astype(jnp.int32)
-    pair_flow, tile = pair_flows(
-        notlast, fwd_offset, after, after_low, after_high, own_patch, own_window, bwd_offset, valid
+    pair_flow, tiles = pair_flows(
+        sec_size * tile_size, notlast, fwd_offset, after, after_low, after_high, own_patch, own_window, bwd_offset, valid
     )
-    devices = sec_size * tile_size
-    everywhere = lax.all_to_all(jnp.broadcast_to(tile[None], (devices,) + tile.shape), ("sec", "tile"), 0, 0)
+    everywhere = lax.all_to_all(tiles, ("sec", "tile"), 0, 0)
     everywhere = (
-        everywhere.reshape(sec_size, tile_size, sec_dev, rows, LANES)
+        everywhere.reshape(sec_size, tile_size, sec_dev, 2, LANES)
         .transpose(0, 2, 1, 3, 4)
-        .reshape(sections, tile_size * rows, LANES)
+        .reshape(sections * tile_size, 2, LANES)
     )
-    where = jnp.stack([place, lax.axis_index("tile") * rows]).astype(jnp.int32)
+    where = (place * tile_size + lax.axis_index("tile")).astype(jnp.int32).reshape(1)
     mesh_shift = pl.pallas_call(
-        mesh_kernel,
+        functools.partial(mesh_kernel, tile_size),
         out_shape=jax.ShapeDtypeStruct(pair_flow.shape, F32),
         in_specs=[SCALARS, pl.BlockSpec(memory_space=pltpu.VMEM)],
         out_specs=pl.BlockSpec(memory_space=pltpu.VMEM),
-        scratch_shapes=[pltpu.VMEM((sections, tile_size * rows, LANES), F32)],
         compiler_params=pltpu.CompilerParams(vmem_limit_bytes=8 * 1024 * 1024),
         name="relax",
     )(where, everywhere)

time: 61.9 us -> 59.6 us (0.963)
  local copies, waits for them, and re-layouts: 6.86 us -> 2.8 us
  starting transfers between devices: 17.5 us -> 19.9 us
  waiting for transfers between devices: 8.33 us -> 7.3 us
    unnamed x26 -> x20, local copies, waits for them, and re-layouts: 5.42 us -> 2.01 us
    all_to_all x1, starting transfers between devices: 8.45 us -> 10.7 us  [body(): everywhere = lax.all_to_all(tiles, ('sec', 'tile'), 0, 0)]
    all_to_all x1, waiting for transfers between devices: 8.32 us -> 7.29 us  [body(): everywhere = lax.all_to_all(tiles, ('sec', 'tile'), 0, 0)]
    pallas_call x1, Pallas kernels: 4.86 us -> 5.75 us  [patch_spectra(): pl.pallas_call(patch_kernel, grid=(sec_dev, pairs), out_shape=shape, in_s...]
    broadcast_in_dim x1 -> x0, local copies, waits for them, and re-layouts: 0.65 us -> none  [body(): jnp.broadcast_to(tile[None], (devices,) + tile.shape)]
  transfers between devices with their start and end apart: 5 -> 5, of which waited for: 1 -> 1; matrix products, arithmetic and copies ran while one was open for 1% -> 1% of each run, Pallas kernels for 18% -> 20%
where the time goes in v3:
time: 59.6 us; the launch traced here: 59.3 us
  Pallas kernels  28.4 us (48%)
  starting transfers between devices  19.9 us (33%)
  waiting for transfers between devices  7.3 us (12%)
  local copies, waits for them, and re-layouts  2.8 us (5%)
  between operations  0.87 us (1%)
    pallas_call x1, Pallas kernels, pair_flows(): pl.pallas_call(pair_kernel, grid=(sec_dev, pairs), out_shape=(flow_shape,...  15.2 us
    all_to_all x1, starting transfers between devices, body(): everywhere = lax.all_to_all(tiles, ('sec', 'tile'), 0, 0)  10.7 us
    all_to_all x1, waiting for transfers between devices, body(): everywhere = lax.all_to_all(tiles, ('sec', 'tile'), 0, 0)  7.29 us
    pallas_call x1, Pallas kernels, window_spectra(): pl.pallas_call(window_kernel, grid=(sec_dev, pairs), out_shape=shape, in_...  6.28 us
    pallas_call x1, Pallas kernels, patch_spectra(): pl.pallas_call(patch_kernel, grid=(sec_dev, pairs), out_shape=shape, in_s...  5.75 us
    ppermute x1, starting transfers between devices, body(): low = lax.ppermute(image[:, -OFFMAX:], 'tile', up)  4.92 us
    unnamed x20, local copies, waits for them, and re-layouts  2.01 us
    ppermute x1, starting transfers between devices, body(): lax.ppermute(jnp.concatenate([low[:1], high[:1]], 1), 'sec', earlier)  1.56 us
  transfers between devices with their start and end apart: 5, of which 1 were waited for; matrix products, arithmetic and copies ran while one was open for 1% of the time, Pallas kernels for 20%

profile of v3, /device:TPU:0, one launch (start us, length us, event | category | flops | bytes accessed | tf_op | source)
XLA Modules:
  0.0 59.3 jit_solution(14262736141699906229)
XLA Ops:
  0.6 1.3 %collective-permute-start = (bf16[1,1024,1024]{2,1,0:T(8,128)(2,1)}, bf16[1,1024,1024]{2,1,0:T(8,128)(2,1)}, u32[]{:S(2)}, u32[]{:S(2)}) collective-permute-start(bf16[1,1024,1024]{2,1,0:T(8,128)(2,1)} %image_ref.3), channel_id=1, source_target_pairs={{4,0},{8,4},{12,8},{16,12},{20,16},{24,20},{28,24},{5,1},{9,5},{13... | collective-permute-start | bytes 6291464 | tf_op jit(solution)/shard_map/ppermute | solution.py:507
  1.9 0.8 %fusion = (bf16[1,16,1024]{2,1,0:T(8,128)(2,1)S(1)}, bf16[1,16,1024]{2,1,0:T(8,128)(2,1)S(1)}) fusion(bf16[1,1024,1024]{2,1,0:T(8,128)(2,1)} %image_ref.3), kind=kLoop, calls=%fused_computation.1 | loop fusion | bytes 131072 | tf_op jit(solution)/shard_map/slice | solution.py:510
  2.7 4.9 %collective-permute-start.1 = (bf16[1,16,1024]{2,1,0:T(8,128)(2,1)S(1)}, bf16[1,16,1024]{2,1,0:T(8,128)(2,1)S(1)}, u32[]{:S(2)}, u32[]{:S(2)}) collective-permute-start(bf16[1,16,1024]{2,1,0:T(8,128)(2,1)S(1)} %get-tuple-element.6), channel_id=1, source_target_pairs={{0,1},{1,2},{2,3},{4,5},{5,6},{6,7},{8,9},{9,10},{10,11},{12,13},{... | collective-permute-start | bytes 98312 | tf_op jit(solution)/shard_map/ppermute | solution.py:510
  7.6 0.0 copy-start
  7.7 0.0 copy-start.2
  7.7 0.0 copy-start.4
  7.7 0.0 copy-start.5
  7.7 1.4 %collective-permute-start.2 = (bf16[1,16,1024]{2,1,0:T(8,128)(2,1)S(1)}, bf16[1,16,1024]{2,1,0:T(8,128)(2,1)S(1)}, u32[]{:S(2)}, u32[]{:S(2)}) collective-permute-start(bf16[1,16,1024]{2,1,0:T(8,128)(2,1)S(1)} %get-tuple-element.7), channel_id=1, source_target_pairs={{1,0},{2,1},{3,2},{5,4},{6,5},{7,6},{9,8},{10,9},{11,10},{13,12},{... | collective-permute-start | bytes 98312 | tf_op jit(solution)/shard_map/ppermute | solution.py:511
  9.1 5.8 %patch_spectra.1.own_patch = f32[1,4,8,128,256]{4,3,2,1,0:T(8,128)S(1)} custom-call(bf16[1,1024,1024]{2,1,0:T(8,128)(2,1)} %image_ref.3, bf16[512,256]{1,0:T(8,128)(2,1)} %constant.22.clone.along_ref, bf16[256,256]{1,0:T(8,128)(2,1)} %constant.23.clone.down_ref), custom_call_target="tpu_custom_call" | custom-call | flops 5000000000 | bytes 10000000 | tf_op jit(solution)/shard_map/patch_spectra/pallas_call | solution.py:410
  14.9 0.0 copy-start.8
  14.9 1.9 %copy-done.8 = f32[1,4,8,128,256]{4,3,2,1,0:T(8,128)} copy-done((f32[1,4,8,128,256]{4,3,2,1,0:T(8,128)}, f32[1,4,8,128,256]{4,3,2,1,0:T(8,128)S(1)}, u32[]{:S(2)}) %copy-start.8) | copy-done | bytes 4194328
  16.8 0.0 collective-permute-done.1.low_ref
  16.8 0.0 collective-permute-done.2.high_ref
  16.9 0.0 copy-start.1
  16.9 0.0 copy-start.3
  16.9 0.0 copy-start.6
  16.9 0.0 copy-start.7
  16.9 0.0 copy-start.9
  16.9 1.6 %collective-permute-start.3 = (bf16[1,32,1024]{2,1,0:T(8,128)(2,1)S(1)}, bf16[1,32,1024]{2,1,0:T(8,128)(2,1)S(1)}, u32[]{:S(2)}, u32[]{:S(2)}) collective-permute-start(bf16[1,32,1024]{2,1,0:T(8,128)(2,1)S(1)} %pad_maximum_fusion), channel_id=1, source_target_pairs={{4,0},{8,4},{12,8},{16,12},{20,16},{24,20},{28,24},{5,1},{9,5},{13... | collective-permute-start | bytes 196616 | tf_op jit(solution)/shard_map/ppermute | solution.py:512
  18.5 0.0 copy-done
  18.5 0.0 copy-done.2
  18.5 0.0 copy-done.4
  18.5 0.0 copy-done.5
  18.5 6.3 %window_spectra.1.own_window = f32[1,4,8,128,256]{4,3,2,1,0:T(8,128)S(1)} custom-call(s32[1,2,8,8]{3,2,1,0:T(8,128)S(1)} %copy-done.2, bf16[1,1024,1024]{2,1,0:T(8,128)(2,1)S(1)} %copy-done, bf16[1,16,1024]{2,1,0:T(8,128)(2,1)S(1)} %collective-permute-done.1.low_ref, bf16[1,16,1024]{2,1,0:T(8,128)(2,1)S(1)} %collective-permute-done.2.high_ref, ...), custom_call_target="tpu_custom_call" | custom-call | flops 5000000000 | bytes 10000000 | tf_op jit(solution)/shard_map/window_spectra/pallas_call | solution.py:431
  24.8 0.0 collective-permute-done.3
  24.8 0.0 collective-permute-done.image_ref
  24.8 0.0 copy-done.1
  24.9 0.0 copy-done.3
  24.9 15.2 %pair_flows.1 = (f32[1,2,8,8]{3,2,1,0:T(8,128)}, f32[32,1,2,128]{3,2,1,0:T(2,128)}) custom-call(s32[1]{0:T(128)} %bitcast.place_ref, s32[1,2,8,8]{3,2,1,0:T(8,128)S(1)} %copy-done.1, bf16[1,1024,1024]{2,1,0:T(8,128)(2,1)} %collective-permute-done.image_ref, bf16[1,16,1024]{2,1,0:T(8,128)(2,1)S(1)} %get-tuple-element.9.low_ref, ...), custom_call_target="tpu_custom_call" | custom-call | flops 20000000000 | bytes 10000000 | tf_op jit(solution)/shard_map/pair_flows/pallas_call | solution.py:462
  40.1 10.7 %all-to-all-start = ((f32[32,1,2,128]{3,2,1,0:T(2,128)}), f32[32,1,2,128]{3,2,1,0:T(2,128)S(1)}, u32[]{:S(2)}, u32[]{:S(2)}) async-start(f32[32,1,2,128]{3,2,1,0:T(2,128)} %get-tuple-element.5), calls=%async_computation | async-start | bytes 65536 | tf_op jit(solution)/shard_map/all_to_all | solution.py:524
  50.9 7.3 %all-to-all-done = f32[32,1,2,128]{3,2,1,0:T(2,128)S(1)} async-done(((f32[32,1,2,128]{3,2,1,0:T(2,128)}), f32[32,1,2,128]{3,2,1,0:T(2,128)S(1)}, u32[]{:S(2)}, u32[]{:S(2)}) %all-to-all-start) | async-done | bytes 32800 | tf_op jit(solution)/shard_map/all_to_all | solution.py:524
  58.2 1.1 %relax.1 = f32[1,2,8,8]{3,2,1,0:T(8,128)} custom-call(s32[1]{0:T(128)} %bitcast.1.place_ref, f32[32,2,128]{2,1,0:T(2,128)S(1)} %bitcast.3), custom_call_target="tpu_custom_call" | custom-call | tf_op jit(solution)/shard_map/relax/pallas_call | solution.py:531
  (5 shorter events, 0.0 us)
Async XLA Ops:
  0.6 24.2 %collective-permute-start = (bf16[1,1024,1024]{2,1,0:T(8,128)(2,1)}, bf16[1,1024,1024]{2,1,0:T(8,128)(2,1)}, u32[]{:S(2)}, u32[]{:S(2)}) collective-permute-start(bf16[1,1024,1024]{2,1,0:T(8,128)(2,1)} %image_ref.3), channel_id=1, source_target_pairs={{4,0},{8,4},{12,8},{16,12},{20,16},{24,20},{28,24},{5,1},{9,5},{13... | collective-permute-start | bytes 6291464 | tf_op jit(solution)/shard_map/ppermute | solution.py:507
  2.7 14.1 %collective-permute-start.1 = (bf16[1,16,1024]{2,1,0:T(8,128)(2,1)S(1)}, bf16[1,16,1024]{2,1,0:T(8,128)(2,1)S(1)}, u32[]{:S(2)}, u32[]{:S(2)}) collective-permute-start(bf16[1,16,1024]{2,1,0:T(8,128)(2,1)S(1)} %get-tuple-element.6), channel_id=1, source_target_pairs={{0,1},{1,2},{2,3},{4,5},{5,6},{6,7},{8,9},{9,10},{10,11},{12,13},{... | collective-permute-start | bytes 98312 | tf_op jit(solution)/shard_map/ppermute | solution.py:510
  7.6 10.8 %copy-start = (bf16[1,1024,1024]{2,1,0:T(8,128)(2,1)S(1)}, bf16[1,1024,1024]{2,1,0:T(8,128)(2,1)}, u32[]{:S(2)}) copy-start(bf16[1,1024,1024]{2,1,0:T(8,128)(2,1)} %image_ref.3) | copy-start | bytes 6291460
  7.7 10.8 %copy-start.2 = (s32[1,2,8,8]{3,2,1,0:T(8,128)S(1)}, s32[1,2,8,8]{3,2,1,0:T(8,128)}, u32[]{:S(2)}) copy-start(s32[1,2,8,8]{3,2,1,0:T(8,128)} %bwd_ref.1) | copy-start | bytes 1540
  7.7 10.8 %copy-start.4 = (bf16[512,256]{1,0:T(8,128)(2,1)S(1)}, bf16[512,256]{1,0:T(8,128)(2,1)}, u32[]{:S(2)}) copy-start(bf16[512,256]{1,0:T(8,128)(2,1)} %constant.22.clone.along_ref) | copy-start | bytes 786436
  7.7 10.8 %copy-start.5 = (bf16[256,256]{1,0:T(8,128)(2,1)S(1)}, bf16[256,256]{1,0:T(8,128)(2,1)}, u32[]{:S(2)}) copy-start(bf16[256,256]{1,0:T(8,128)(2,1)} %constant.23.clone.down_ref) | copy-start | bytes 393220
  7.7 9.2 %collective-permute-start.2 = (bf16[1,16,1024]{2,1,0:T(8,128)(2,1)S(1)}, bf16[1,16,1024]{2,1,0:T(8,128)(2,1)S(1)}, u32[]{:S(2)}, u32[]{:S(2)}) collective-permute-start(bf16[1,16,1024]{2,1,0:T(8,128)(2,1)S(1)} %get-tuple-element.7), channel_id=1, source_target_pairs={{1,0},{2,1},{3,2},{5,4},{6,5},{7,6},{9,8},{10,9},{11,10},{13,12},{... | collective-permute-start | bytes 98312 | tf_op jit(solution)/shard_map/ppermute | solution.py:511
  14.9 2.0 %copy-start.8 = (f32[1,4,8,128,256]{4,3,2,1,0:T(8,128)}, f32[1,4,8,128,256]{4,3,2,1,0:T(8,128)S(1)}, u32[]{:S(2)}) copy-start(f32[1,4,8,128,256]{4,3,2,1,0:T(8,128)S(1)} %patch_spectra.1.own_patch) | copy-start | bytes 12582916
  16.9 8.0 %copy-start.1 = (s32[1,2,8,8]{3,2,1,0:T(8,128)S(1)}, s32[1,2,8,8]{3,2,1,0:T(8,128)}, u32[]{:S(2)}) copy-start(s32[1,2,8,8]{3,2,1,0:T(8,128)} %fwd_ref.1) | copy-start | bytes 1540
  16.9 8.0 %copy-start.3 = (s32[1,8,8]{2,1,0:T(8,128)S(1)}, s32[1,8,8]{2,1,0:T(8,128)}, u32[]{:S(2)}) copy-start(s32[1,8,8]{2,1,0:T(8,128)} %valid_ref.1) | copy-start | bytes 772
  16.9 8.0 %copy-start.6 = (bf16[256,256]{1,0:T(8,128)(2,1)S(1)}, bf16[256,256]{1,0:T(8,128)(2,1)}, u32[]{:S(2)}) copy-start(bf16[256,256]{1,0:T(8,128)(2,1)} %constant.25.clone.cols_ref) | copy-start | bytes 393220
  16.9 8.0 %copy-start.7 = (bf16[128,256]{1,0:T(8,128)(2,1)S(1)}, bf16[128,256]{1,0:T(8,128)(2,1)}, u32[]{:S(2)}) copy-start(bf16[128,256]{1,0:T(8,128)(2,1)} %constant.24.clone.rows_ref) | copy-start | bytes 196612
  16.9 8.0 %copy-start.9 = (f32[1,4,8,128,256]{4,3,2,1,0:T(8,128)S(1)}, f32[1,4,8,128,256]{4,3,2,1,0:T(8,128)}, u32[]{:S(2)}) copy-start(f32[1,4,8,128,256]{4,3,2,1,0:T(8,128)} %copy-done.8) | copy-start | bytes 12582916
  16.9 7.9 %collective-permute-start.3 = (bf16[1,32,1024]{2,1,0:T(8,128)(2,1)S(1)}, bf16[1,32,1024]{2,1,0:T(8,128)(2,1)S(1)}, u32[]{:S(2)}, u32[]{:S(2)}) collective-permute-start(bf16[1,32,1024]{2,1,0:T(8,128)(2,1)S(1)} %pad_maximum_fusion), channel_id=1, source_target_pairs={{4,0},{8,4},{12,8},{16,12},{20,16},{24,20},{28,24},{5,1},{9,5},{13... | collective-permute-start | bytes 196616 | tf_op jit(solution)/shard_map/ppermute | solution.py:512
  40.1 18.0 %all-to-all-start = ((f32[32,1,2,128]{3,2,1,0:T(2,128)}), f32[32,1,2,128]{3,2,1,0:T(2,128)S(1)}, u32[]{:S(2)}, u32[]{:S(2)}) async-start(f32[32,1,2,128]{3,2,1,0:T(2,128)} %get-tuple-element.5), calls=%async_computation | async-start | bytes 65536 | tf_op jit(solution)/shard_map/all_to_all | solution.py:524

commit v4 on v3

--- a/solution.py
+++ b/solution.py
@@ -230,87 +230,101 @@
     own_patch, own_window, fwd_ref, bwd_ref, valid_ref, flow_out, tile_out,
     padded, window, parts, left, right, coef, pieces, sums,
 ):
-    s, c = pl.program_id(0), pl.program_id(1)
+    s = pl.program_id(0)
     rows = image_ref.shape[0] // PATCH
-    pairs = pl.num_programs(1)
-
-    @pl.when(c == 0)
-    def _():
-        fill_padded(padded, image_ref, low_ref, high_ref)
-        for i in range(rows):
-            fill_window_row(window.at[0], padded, off_ref, s, 0, i)
-
-    lanes = pl.ds(pl.multiple_of(c * 2 * LANES, 2 * LANES), 2 * LANES)
-    first_stage(image_ref[:, lanes], along_ref, parts.at[0])
-    first_stage(window[c % 2], along_ref, parts.at[1])
-    following = jnp.minimum(c + 1, pairs - 1)
-
-    def spectra(i):
-        store_coefficients(left.at[i % 2], second_stage(parts[0, i], down_ref))
-        store_coefficients(right.at[i % 2], second_stage(parts[1, i], down_ref))
-
-    def products(i):
-        k = i % 2
+    pairs = own_patch.shape[1]
+    steps = pairs * rows
+
+    def first_image(c):
+        first_stage(image_ref[:, 2 * c * LANES : 2 * (c + 1) * LANES], along_ref, parts.at[c % 2, 0])
+
+    def first_window(c):
+        first_stage(window[c % 2], along_ref, parts.at[c % 2, 1])
+
+    def cut(c, i):
+        fill_window_row(window.at[c % 2], padded, off_ref, s, c, i)
+
+    def spectra(n):
+        c, i = divmod(n, rows)
+        store_coefficients(left.at[n % 2], second_stage(parts[c % 2, 0, i], down_ref))
+        store_coefficients(right.at[n % 2], second_stage(parts[c % 2, 1, i], down_ref))
+
+    def products(n):
+        c, i = divmod(n, rows)
+        k = n % 2
         sums[0, c, i : i + 1, :] = cross(own_patch.at[s, c, i], right.at[k], coef.at[0, k], pieces.at[0, k])
         sums[3, c, i : i + 1, :] = cross(left.at[k], own_window.at[s, c, i], coef.at[1, k], pieces.at[1, k])
 
-    def centroid(i):
+    def centroid(n):
+        c, i = divmod(n, rows)
         for d in range(2):
-            by_row, by_col = moments(coef.at[d, i % 2], pieces.at[d, i % 2], rows_ref, cols_ref)
+            by_row, by_col = moments(coef.at[d, n % 2], pieces.at[d, n % 2], rows_ref, cols_ref)
             sums[3 * d + 1, c, i : i + 1, :] = by_row
             sums[3 * d + 2, c, i : i + 1, :] = by_col
 
+    fill_padded(padded, image_ref, low_ref, high_ref)
+    first_image(0)
+    for i in range(rows):
+        cut(0, i)
+    first_window(0)
     spectra(0)
-    for i in range(rows):
-        if i + 1 < rows:
-            spectra(i + 1)
-        products(i)
-        fill_window_row(window.at[(c + 1) % 2], padded, off_ref, s, following, i)
-        if i:
-            centroid(i - 1)
-    centroid(rows - 1)
-
-    @pl.when(c == pairs - 1)
-    def _():
-        count = 2 * sums.shape[1]
-        lane = lax.broadcasted_iota(jnp.int32, (rows, LANES), 1)
-        gathered = []
-        for k in range(6):
-            value = jnp.zeros((rows, LANES), F32)
-            for p in range(sums.shape[1]):
-                held = sums[k, p]
-                for t in range(2):
-                    mine = (lane >= HALF) if t else (lane < HALF)
-                    value = jnp.where(
-                        lane == 2 * p + t, jnp.sum(jnp.where(mine, held, 0.0), axis=1, keepdims=True), value
-                    )
-            gathered.append(value[:, :count])
-        scale = (2.0 / PATCH) ** 4 * HALF * HALF
-        lag_scale = scale / HALF
-        eps = PATCH * PATCH * 1e-6
-        notlast = place_ref[s].astype(F32)
-        weight = valid_ref[...].astype(F32) * notlast
-        flows = []
-        for comp in range(2):
-            fwd = gathered[1 + comp] * lag_scale / (gathered[0] * scale + eps) + fwd_ref[comp].astype(F32)
-            bwd = gathered[4 + comp] * lag_scale / (gathered[3] * scale + eps) + bwd_ref[comp].astype(F32)
-            flow = 0.5 * (fwd - bwd) * notlast
-            flow_out[comp] = flow
-            flows.append(flow)
-        fill = jnp.zeros((rows, LANES - 4 * count), F32)
-        wide = jnp.concatenate(flows + [weight, weight, fill], axis=1)
-        row = lax.broadcasted_iota(jnp.int32, (rows, LANES), 0)
-        group = 2 * count
-        packed = []
-        for begin in (0, group):
-            line = jnp.zeros((rows, LANES), F32)
-            for i in range(rows):
-                turned = pltpu.roll(wide, (group * i - begin) % LANES, 1)
-                line = jnp.where(jnp.logical_and(row == i, lane // group == i), turned, line)
-            packed.append(jnp.sum(line, axis=0, keepdims=True))
-        packed = jnp.concatenate(packed, axis=0)
-        for k in range(tile_out.shape[0]):
-            tile_out[k, s] = packed
+    early = max(rows - 2, 1)
+    ready = [i * rows // early for i in range(early + 1)]
+    for n in range(steps):
+        c, i = divmod(n, rows)
+        if c + 1 < pairs and i < early:
+            for r in range(ready[i], ready[i + 1]):
+                cut(c + 1, r)
+            if i == 1:
+                first_image(c + 1)
+            if i == early - 1:
+                first_window(c + 1)
+        if n + 1 < steps:
+            spectra(n + 1)
+        products(n)
+        if n:
+            centroid(n - 1)
+    centroid(steps - 1)
+
+    count = 2 * sums.shape[1]
+    lane = lax.broadcasted_iota(jnp.int32, (rows, LANES), 1)
+    gathered = []
+    for k in range(6):
+        value = jnp.zeros((rows, LANES), F32)
+        for p in range(sums.shape[1]):
+            held = sums[k, p]
+            for t in range(2):
+                mine = (lane >= HALF) if t else (lane < HALF)
+                value = jnp.where(
+                    lane == 2 * p + t, jnp.sum(jnp.where(mine, held, 0.0), axis=1, keepdims=True), value
+                )
+        gathered.append(value[:, :count])
+    scale = (2.0 / PATCH) ** 4 * HALF * HALF
+    lag_scale = scale / HALF
+    eps = PATCH * PATCH * 1e-6
+    notlast = place_ref[s].astype(F32)
+    weight = valid_ref[...].astype(F32) * notlast
+    flows = []
+    for comp in range(2):
+        fwd = gathered[1 + comp] * lag_scale / (gathered[0] * scale + eps) + fwd_ref[comp].astype(F32)
+        bwd = gathered[4 + comp] * lag_scale / (gathered[3] * scale + eps) + bwd_ref[comp].astype(F32)
+        flow = 0.5 * (fwd - bwd) * notlast
+        flow_out[comp] = flow
+        flows.append(flow)
+    fill = jnp.zeros((rows, LANES - 4 * count), F32)
+    wide = jnp.concatenate(flows + [weight, weight, fill], axis=1)
+    row = lax.broadcasted_iota(jnp.int32, (rows, LANES), 0)
+    group = 2 * count
+    packed = []
+    for begin in (0, group):
+        line = jnp.zeros((rows, LANES), F32)
+        for i in range(rows):
+            turned = pltpu.roll(wide, (group * i - begin) % LANES, 1)
+            line = jnp.where(jnp.logical_and(row == i, lane // group == i), turned, line)
+        packed.append(jnp.sum(line, axis=0, keepdims=True))
+    packed = jnp.concatenate(packed, axis=0)
+    for k in range(tile_out.shape[0]):
+        tile_out[k, s] = packed
 
 
 def mesh_kernel(tiles, place_ref, all_ref, shift_out):
@@ -378,11 +392,11 @@
 
 
 def section_spec(shape):
-    return pl.BlockSpec((None,) + shape[1:], lambda s, c: (s,) + (0,) * (len(shape) - 1))
+    return pl.BlockSpec((None,) + shape[1:], lambda s, *_: (s,) + (0,) * (len(shape) - 1))
 
 
 def whole_spec(shape):
-    return pl.BlockSpec(shape, lambda s, c: (0,) * len(shape))
+    return pl.BlockSpec(shape, lambda *_: (0,) * len(shape))
 
 
 SCALARS = pl.BlockSpec(memory_space=pltpu.SMEM)
@@ -461,7 +475,7 @@
     flow_shape = jax.ShapeDtypeStruct((sec_dev, 2, rows, count), F32)
     return pl.pallas_call(
         pair_kernel,
-        grid=(sec_dev, pairs),
+        grid=(sec_dev,),
         out_shape=(flow_shape, jax.ShapeDtypeStruct((devices, sec_dev, 2, LANES), F32)),
         in_specs=[
             SCALARS,
@@ -483,7 +497,7 @@
         scratch_shapes=[
             pltpu.VMEM((height + 2 * OFFMAX + 8, width + 2 * LANES), F32),
             pltpu.VMEM((2, height, 2 * LANES), BF),
-            pltpu.VMEM((2, rows, 2 * PATCH, 2 * PATCH), BF),
+            pltpu.VMEM((2, 2, rows, 2 * PATCH, 2 * PATCH), BF),
             pltpu.VMEM((2, PATCH, 2 * PATCH), F32),
             pltpu.VMEM((2, PATCH, 2 * PATCH), F32),
             pltpu.VMEM((2, 2, PATCH, 2 * PATCH), F32),

time: 59.6 us -> 58.1 us (0.975)
  Pallas kernels: 28.4 us -> 27 us
    pallas_call x1, Pallas kernels: 15.2 us -> 13.7 us  [pair_flows(): pl.pallas_call(pair_kernel, grid=(sec_dev,), out_shape=(flow_shape, jax.S...]
  transfers between devices with their start and end apart: 5 -> 5, of which waited for: 1 -> 1; matrix products, arithmetic and copies ran while one was open for 1% -> 1% of each run, Pallas kernels for 20% -> 21%
where the time goes in v4:
time: 58.1 us; the launch traced here: 57.7 us
  Pallas kernels  27 us (46%)
  starting transfers between devices  19.8 us (34%)
  waiting for transfers between devices  7.3 us (13%)
  local copies, waits for them, and re-layouts  2.8 us (5%)
  between operations  0.87 us (1%)
    pallas_call x1, Pallas kernels, pair_flows(): pl.pallas_call(pair_kernel, grid=(sec_dev,), out_shape=(flow_shape, jax.S...  13.7 us
    all_to_all x1, starting transfers between devices, body(): everywhere = lax.all_to_all(tiles, ('sec', 'tile'), 0, 0)  10.6 us
    all_to_all x1, waiting for transfers between devices, body(): everywhere = lax.all_to_all(tiles, ('sec', 'tile'), 0, 0)  7.29 us
    pallas_call x1, Pallas kernels, window_spectra(): pl.pallas_call(window_kernel, grid=(sec_dev, pairs), out_shape=shape, in_...  6.27 us
    pallas_call x1, Pallas kernels, patch_spectra(): pl.pallas_call(patch_kernel, grid=(sec_dev, pairs), out_shape=shape, in_s...  5.86 us
    ppermute x1, starting transfers between devices, body(): low = lax.ppermute(image[:, -OFFMAX:], 'tile', up)  4.92 us
    unnamed x20, local copies, waits for them, and re-layouts  2.01 us
    ppermute x1, starting transfers between devices, body(): lax.ppermute(jnp.concatenate([low[:1], high[:1]], 1), 'sec', earlier)  1.56 us
  transfers between devices with their start and end apart: 5, of which 1 were waited for; matrix products, arithmetic and copies ran while one was open for 1% of the time, Pallas kernels for 21%

profile of v4, /device:TPU:0, one launch (start us, length us, event | category | flops | bytes accessed | tf_op | source)
XLA Modules:
  0.0 57.7 jit_solution(13859285368567301846)
XLA Ops:
  0.6 1.3 %collective-permute-start = (bf16[1,1024,1024]{2,1,0:T(8,128)(2,1)}, bf16[1,1024,1024]{2,1,0:T(8,128)(2,1)}, u32[]{:S(2)}, u32[]{:S(2)}) collective-permute-start(bf16[1,1024,1024]{2,1,0:T(8,128)(2,1)} %image_ref.3), channel_id=1, source_target_pairs={{4,0},{8,4},{12,8},{16,12},{20,16},{24,20},{28,24},{5,1},{9,5},{13... | collective-permute-start | bytes 6291464 | tf_op jit(solution)/shard_map/ppermute | solution.py:521
  1.9 0.8 %fusion = (bf16[1,16,1024]{2,1,0:T(8,128)(2,1)S(1)}, bf16[1,16,1024]{2,1,0:T(8,128)(2,1)S(1)}) fusion(bf16[1,1024,1024]{2,1,0:T(8,128)(2,1)} %image_ref.3), kind=kLoop, calls=%fused_computation.1 | loop fusion | bytes 131072 | tf_op jit(solution)/shard_map/slice | solution.py:524
  2.7 4.9 %collective-permute-start.1 = (bf16[1,16,1024]{2,1,0:T(8,128)(2,1)S(1)}, bf16[1,16,1024]{2,1,0:T(8,128)(2,1)S(1)}, u32[]{:S(2)}, u32[]{:S(2)}) collective-permute-start(bf16[1,16,1024]{2,1,0:T(8,128)(2,1)S(1)} %get-tuple-element.6), channel_id=1, source_target_pairs={{0,1},{1,2},{2,3},{4,5},{5,6},{6,7},{8,9},{9,10},{10,11},{12,13},{... | collective-permute-start | bytes 98312 | tf_op jit(solution)/shard_map/ppermute | solution.py:524
  7.6 0.0 copy-start
  7.7 0.0 copy-start.2
  7.7 0.0 copy-start.4
  7.7 0.0 copy-start.5
  7.7 1.4 %collective-permute-start.2 = (bf16[1,16,1024]{2,1,0:T(8,128)(2,1)S(1)}, bf16[1,16,1024]{2,1,0:T(8,128)(2,1)S(1)}, u32[]{:S(2)}, u32[]{:S(2)}) collective-permute-start(bf16[1,16,1024]{2,1,0:T(8,128)(2,1)S(1)} %get-tuple-element.7), channel_id=1, source_target_pairs={{1,0},{2,1},{3,2},{5,4},{6,5},{7,6},{9,8},{10,9},{11,10},{13,12},{... | collective-permute-start | bytes 98312 | tf_op jit(solution)/shard_map/ppermute | solution.py:525
  9.1 5.9 %patch_spectra.1.own_patch = f32[1,4,8,128,256]{4,3,2,1,0:T(8,128)S(1)} custom-call(bf16[1,1024,1024]{2,1,0:T(8,128)(2,1)} %image_ref.3, bf16[512,256]{1,0:T(8,128)(2,1)} %constant.22.clone.along_ref, bf16[256,256]{1,0:T(8,128)(2,1)} %constant.23.clone.down_ref), custom_call_target="tpu_custom_call" | custom-call | flops 5000000000 | bytes 10000000 | tf_op jit(solution)/shard_map/patch_spectra/pallas_call | solution.py:424
  15.0 0.0 copy-start.8
  15.0 1.9 %copy-done.8 = f32[1,4,8,128,256]{4,3,2,1,0:T(8,128)} copy-done((f32[1,4,8,128,256]{4,3,2,1,0:T(8,128)}, f32[1,4,8,128,256]{4,3,2,1,0:T(8,128)S(1)}, u32[]{:S(2)}) %copy-start.8) | copy-done | bytes 4194328
  16.9 0.0 collective-permute-done.1.low_ref
  17.0 0.0 collective-permute-done.2.high_ref
  17.0 0.0 copy-start.1
  17.0 0.0 copy-start.3
  17.0 0.0 copy-start.6
  17.0 0.0 copy-start.7
  17.0 0.0 copy-start.9
  17.0 1.6 %collective-permute-start.3 = (bf16[1,32,1024]{2,1,0:T(8,128)(2,1)S(1)}, bf16[1,32,1024]{2,1,0:T(8,128)(2,1)S(1)}, u32[]{:S(2)}, u32[]{:S(2)}) collective-permute-start(bf16[1,32,1024]{2,1,0:T(8,128)(2,1)S(1)} %pad_maximum_fusion), channel_id=1, source_target_pairs={{4,0},{8,4},{12,8},{16,12},{20,16},{24,20},{28,24},{5,1},{9,5},{13... | collective-permute-start | bytes 196616 | tf_op jit(solution)/shard_map/ppermute | solution.py:526
  18.6 0.0 copy-done
  18.6 6.3 %window_spectra.1.own_window = f32[1,4,8,128,256]{4,3,2,1,0:T(8,128)S(1)} custom-call(s32[1,2,8,8]{3,2,1,0:T(8,128)S(1)} %copy-done.2, bf16[1,1024,1024]{2,1,0:T(8,128)(2,1)S(1)} %copy-done, bf16[1,16,1024]{2,1,0:T(8,128)(2,1)S(1)} %collective-permute-done.1.low_ref, bf16[1,16,1024]{2,1,0:T(8,128)(2,1)S(1)} %collective-permute-done.2.high_ref, ...), custom_call_target="tpu_custom_call" | custom-call | flops 5000000000 | bytes 10000000 | tf_op jit(solution)/shard_map/window_spectra/pallas_call | solution.py:445
  24.9 0.0 collective-permute-done.3
  24.9 0.0 collective-permute-done.image_ref
  24.9 0.0 copy-done.1
  25.0 0.0 copy-done.3
  25.0 0.0 copy-done.6
  25.0 0.0 copy-done.7
  25.0 0.0 copy-done.9
  25.0 13.7 %pair_flows.1 = (f32[1,2,8,8]{3,2,1,0:T(8,128)}, f32[32,1,2,128]{3,2,1,0:T(2,128)}) custom-call(s32[1]{0:T(128)} %bitcast.place_ref, s32[1,2,8,8]{3,2,1,0:T(8,128)S(1)} %copy-done.1, bf16[1,1024,1024]{2,1,0:T(8,128)(2,1)} %collective-permute-done.image_ref, bf16[1,16,1024]{2,1,0:T(8,128)(2,1)S(1)} %get-tuple-element.9.low_ref, ...), custom_call_target="tpu_custom_call" | custom-call | flops 20000000000 | bytes 10000000 | tf_op jit(solution)/shard_map/pair_flows/pallas_call | solution.py:476
  38.7 10.6 %all-to-all-start = ((f32[32,1,2,128]{3,2,1,0:T(2,128)}), f32[32,1,2,128]{3,2,1,0:T(2,128)S(1)}, u32[]{:S(2)}, u32[]{:S(2)}) async-start(f32[32,1,2,128]{3,2,1,0:T(2,128)} %get-tuple-element.5), calls=%async_computation | async-start | bytes 65536 | tf_op jit(solution)/shard_map/all_to_all | solution.py:538
  49.3 7.3 %all-to-all-done = f32[32,1,2,128]{3,2,1,0:T(2,128)S(1)} async-done(((f32[32,1,2,128]{3,2,1,0:T(2,128)}), f32[32,1,2,128]{3,2,1,0:T(2,128)S(1)}, u32[]{:S(2)}, u32[]{:S(2)}) %all-to-all-start) | async-done | bytes 32800 | tf_op jit(solution)/shard_map/all_to_all | solution.py:538
  56.6 1.1 %relax.1 = f32[1,2,8,8]{3,2,1,0:T(8,128)} custom-call(s32[1]{0:T(128)} %bitcast.1.place_ref, f32[32,2,128]{2,1,0:T(2,128)S(1)} %bitcast.3), custom_call_target="tpu_custom_call" | custom-call | tf_op jit(solution)/shard_map/relax/pallas_call | solution.py:545
  (5 shorter events, 0.0 us)
Async XLA Ops:
  0.6 24.3 %collective-permute-start = (bf16[1,1024,1024]{2,1,0:T(8,128)(2,1)}, bf16[1,1024,1024]{2,1,0:T(8,128)(2,1)}, u32[]{:S(2)}, u32[]{:S(2)}) collective-permute-start(bf16[1,1024,1024]{2,1,0:T(8,128)(2,1)} %image_ref.3), channel_id=1, source_target_pairs={{4,0},{8,4},{12,8},{16,12},{20,16},{24,20},{28,24},{5,1},{9,5},{13... | collective-permute-start | bytes 6291464 | tf_op jit(solution)/shard_map/ppermute | solution.py:521
  2.7 14.2 %collective-permute-start.1 = (bf16[1,16,1024]{2,1,0:T(8,128)(2,1)S(1)}, bf16[1,16,1024]{2,1,0:T(8,128)(2,1)S(1)}, u32[]{:S(2)}, u32[]{:S(2)}) collective-permute-start(bf16[1,16,1024]{2,1,0:T(8,128)(2,1)S(1)} %get-tuple-element.6), channel_id=1, source_target_pairs={{0,1},{1,2},{2,3},{4,5},{5,6},{6,7},{8,9},{9,10},{10,11},{12,13},{... | collective-permute-start | bytes 98312 | tf_op jit(solution)/shard_map/ppermute | solution.py:524
  7.6 11.0 %copy-start = (bf16[1,1024,1024]{2,1,0:T(8,128)(2,1)S(1)}, bf16[1,1024,1024]{2,1,0:T(8,128)(2,1)}, u32[]{:S(2)}) copy-start(bf16[1,1024,1024]{2,1,0:T(8,128)(2,1)} %image_ref.3) | copy-start | bytes 6291460
  7.7 10.9 %copy-start.2 = (s32[1,2,8,8]{3,2,1,0:T(8,128)S(1)}, s32[1,2,8,8]{3,2,1,0:T(8,128)}, u32[]{:S(2)}) copy-start(s32[1,2,8,8]{3,2,1,0:T(8,128)} %bwd_ref.1) | copy-start | bytes 1540
  7.7 10.9 %copy-start.4 = (bf16[512,256]{1,0:T(8,128)(2,1)S(1)}, bf16[512,256]{1,0:T(8,128)(2,1)}, u32[]{:S(2)}) copy-start(bf16[512,256]{1,0:T(8,128)(2,1)} %constant.22.clone.along_ref) | copy-start | bytes 786436
  7.7 10.9 %copy-start.5 = (bf16[256,256]{1,0:T(8,128)(2,1)S(1)}, bf16[256,256]{1,0:T(8,128)(2,1)}, u32[]{:S(2)}) copy-start(bf16[256,256]{1,0:T(8,128)(2,1)} %constant.23.clone.down_ref) | copy-start | bytes 393220
  7.7 9.3 %collective-permute-start.2 = (bf16[1,16,1024]{2,1,0:T(8,128)(2,1)S(1)}, bf16[1,16,1024]{2,1,0:T(8,128)(2,1)S(1)}, u32[]{:S(2)}, u32[]{:S(2)}) collective-permute-start(bf16[1,16,1024]{2,1,0:T(8,128)(2,1)S(1)} %get-tuple-element.7), channel_id=1, source_target_pairs={{1,0},{2,1},{3,2},{5,4},{6,5},{7,6},{9,8},{10,9},{11,10},{13,12},{... | collective-permute-start | bytes 98312 | tf_op jit(solution)/shard_map/ppermute | solution.py:525
  15.0 2.0 %copy-start.8 = (f32[1,4,8,128,256]{4,3,2,1,0:T(8,128)}, f32[1,4,8,128,256]{4,3,2,1,0:T(8,128)S(1)}, u32[]{:S(2)}) copy-start(f32[1,4,8,128,256]{4,3,2,1,0:T(8,128)S(1)} %patch_spectra.1.own_patch) | copy-start | bytes 12582916
  17.0 8.0 %copy-start.1 = (s32[1,2,8,8]{3,2,1,0:T(8,128)S(1)}, s32[1,2,8,8]{3,2,1,0:T(8,128)}, u32[]{:S(2)}) copy-start(s32[1,2,8,8]{3,2,1,0:T(8,128)} %fwd_ref.1) | copy-start | bytes 1540
  17.0 8.0 %copy-start.3 = (s32[1,8,8]{2,1,0:T(8,128)S(1)}, s32[1,8,8]{2,1,0:T(8,128)}, u32[]{:S(2)}) copy-start(s32[1,8,8]{2,1,0:T(8,128)} %valid_ref.1) | copy-start | bytes 772
  17.0 8.0 %copy-start.6 = (bf16[256,256]{1,0:T(8,128)(2,1)S(1)}, bf16[256,256]{1,0:T(8,128)(2,1)}, u32[]{:S(2)}) copy-start(bf16[256,256]{1,0:T(8,128)(2,1)} %constant.25.clone.cols_ref) | copy-start | bytes 393220
  17.0 8.0 %copy-start.7 = (bf16[128,256]{1,0:T(8,128)(2,1)S(1)}, bf16[128,256]{1,0:T(8,128)(2,1)}, u32[]{:S(2)}) copy-start(bf16[128,256]{1,0:T(8,128)(2,1)} %constant.24.clone.rows_ref) | copy-start | bytes 196612
  17.0 8.0 %copy-start.9 = (f32[1,4,8,128,256]{4,3,2,1,0:T(8,128)S(1)}, f32[1,4,8,128,256]{4,3,2,1,0:T(8,128)}, u32[]{:S(2)}) copy-start(f32[1,4,8,128,256]{4,3,2,1,0:T(8,128)} %copy-done.8) | copy-start | bytes 12582916
  17.0 7.9 %collective-permute-start.3 = (bf16[1,32,1024]{2,1,0:T(8,128)(2,1)S(1)}, bf16[1,32,1024]{2,1,0:T(8,128)(2,1)S(1)}, u32[]{:S(2)}, u32[]{:S(2)}) collective-permute-start(bf16[1,32,1024]{2,1,0:T(8,128)(2,1)S(1)} %pad_maximum_fusion), channel_id=1, source_target_pairs={{4,0},{8,4},{12,8},{16,12},{20,16},{24,20},{28,24},{5,1},{9,5},{13... | collective-permute-start | bytes 196616 | tf_op jit(solution)/shard_map/ppermute | solution.py:526
  38.7 17.9 %all-to-all-start = ((f32[32,1,2,128]{3,2,1,0:T(2,128)}), f32[32,1,2,128]{3,2,1,0:T(2,128)S(1)}, u32[]{:S(2)}, u32[]{:S(2)}) async-start(f32[32,1,2,128]{3,2,1,0:T(2,128)} %get-tuple-element.5), calls=%async_computation | async-start | bytes 65536 | tf_op jit(solution)/shard_map/all_to_all | solution.py:538

commit v5 on v4

--- a/solution.py
+++ b/solution.py
@@ -327,7 +327,7 @@
         tile_out[k, s] = packed
 
 
-def mesh_kernel(tiles, place_ref, all_ref, shift_out):
+def mesh_kernel(tiles, all_ref, shift_out):
     bands = all_ref.shape[0]
     sec_dev, _, rows, count = shift_out.shape
     group = 2 * count
@@ -381,8 +381,9 @@
         shift = shift + 0.25 * (plane + between)
     mine_line = lax.broadcasted_iota(jnp.int32, (bands, LANES), 0)
     row = lax.broadcasted_iota(jnp.int32, (rows, LANES), 0)
+    place = lax.axis_index("sec") * sec_dev * tiles + lax.axis_index("tile")
     for k in range(sec_dev):
-        mine = jnp.sum(jnp.where(mine_line == place_ref[0] + k * tiles, shift, 0.0), axis=0, keepdims=True)
+        mine = jnp.sum(jnp.where(mine_line == place + k * tiles, shift, 0.0), axis=0, keepdims=True)
         spread = jnp.zeros((rows, LANES), F32)
         wide = jnp.broadcast_to(mine, (rows, LANES))
         for i in range(rows):
@@ -541,15 +542,14 @@
         .transpose(0, 2, 1, 3, 4)
         .reshape(sections * tile_size, 2, LANES)
     )
-    where = (place * tile_size + lax.axis_index("tile")).astype(jnp.int32).reshape(1)
     mesh_shift = pl.pallas_call(
         functools.partial(mesh_kernel, tile_size),
         out_shape=jax.ShapeDtypeStruct(pair_flow.shape, F32),
-        in_specs=[SCALARS, pl.BlockSpec(memory_space=pltpu.VMEM)],
+        in_specs=[pl.BlockSpec(memory_space=pltpu.VMEM)],
         out_specs=pl.BlockSpec(memory_space=pltpu.VMEM),
         compiler_params=pltpu.CompilerParams(vmem_limit_bytes=8 * 1024 * 1024),
         name="relax",
-    )(where, everywhere)
+    )(everywhere)
     return pair_flow, mesh_shift
 
 

time: 58.1 us -> 57.7 us (level)
  blocking collectives: 0 us -> 17.7 us
  starting transfers between devices: 19.8 us -> 9.19 us
  waiting for transfers between devices: 7.3 us -> 0.01 us
    all_to_all x0 -> x1, blocking collectives: none -> 17.7 us  [body(): everywhere = lax.all_to_all(tiles, ('sec', 'tile'), 0, 0)]
    all_to_all x1 -> x0, starting transfers between devices: 10.6 us -> none  [body(): everywhere = lax.all_to_all(tiles, ('sec', 'tile'), 0, 0)]
    all_to_all x1 -> x0, waiting for transfers between devices: 7.29 us -> none  [body(): everywhere = lax.all_to_all(tiles, ('sec', 'tile'), 0, 0)]
  transfers between devices with their start and end apart: 5 -> 4, of which waited for: 1 -> 0; matrix products, arithmetic and copies ran while one was open for 1% -> 1% of each run, Pallas kernels for 21% -> 21%
where the time goes in v5:
time: 57.7 us; the launch traced here: 57.4 us
  Pallas kernels  26.8 us (46%)
  blocking collectives  17.7 us (31%)
  starting transfers between devices  9.19 us (16%)
  local copies, waits for them, and re-layouts  2.81 us (5%)
  between operations  0.86 us (1%)
    all_to_all x1, blocking collectives, body(): everywhere = lax.all_to_all(tiles, ('sec', 'tile'), 0, 0)  17.7 us
    pallas_call x1, Pallas kernels, pair_flows(): pl.pallas_call(pair_kernel, grid=(sec_dev,), out_shape=(flow_shape, jax.S...  13.5 us
    pallas_call x1, Pallas kernels, window_spectra(): pl.pallas_call(window_kernel, grid=(sec_dev, pairs), out_shape=shape, in_...  6.28 us
    pallas_call x1, Pallas kernels, patch_spectra(): pl.pallas_call(patch_kernel, grid=(sec_dev, pairs), out_shape=shape, in_s...  5.86 us
    ppermute x1, starting transfers between devices, body(): low = lax.ppermute(image[:, -OFFMAX:], 'tile', up)  4.92 us
    unnamed x20, local copies, waits for them, and re-layouts  2.02 us
    ppermute x1, starting transfers between devices, body(): lax.ppermute(jnp.concatenate([low[:1], high[:1]], 1), 'sec', earlier)  1.56 us
    ppermute x1, starting transfers between devices, body(): high = lax.ppermute(image[:, :OFFMAX], 'tile', back)  1.42 us
  transfers between devices with their start and end apart: 4, of which 0 were waited for; matrix products, arithmetic and copies ran while one was open for 1% of the time, Pallas kernels for 21%

profile of v5, /device:TPU:0, one launch (start us, length us, event | category | flops | bytes accessed | tf_op | source)
XLA Modules:
  0.0 57.4 jit_solution(16781447435767543690)
XLA Ops:
  0.6 1.3 %collective-permute-start = (bf16[1,1024,1024]{2,1,0:T(8,128)(2,1)}, bf16[1,1024,1024]{2,1,0:T(8,128)(2,1)}, u32[]{:S(2)}, u32[]{:S(2)}) collective-permute-start(bf16[1,1024,1024]{2,1,0:T(8,128)(2,1)} %image_ref.3), channel_id=1, source_target_pairs={{4,0},{8,4},{12,8},{16,12},{20,16},{24,20},{28,24},{5,1},{9,5},{13... | collective-permute-start | bytes 6291464 | tf_op jit(solution)/shard_map/ppermute | solution.py:522
  1.9 0.8 %fusion = (bf16[1,16,1024]{2,1,0:T(8,128)(2,1)S(1)}, bf16[1,16,1024]{2,1,0:T(8,128)(2,1)S(1)}) fusion(bf16[1,1024,1024]{2,1,0:T(8,128)(2,1)} %image_ref.3), kind=kLoop, calls=%fused_computation.1 | loop fusion | bytes 131072 | tf_op jit(solution)/shard_map/slice | solution.py:525
  2.7 4.9 %collective-permute-start.1 = (bf16[1,16,1024]{2,1,0:T(8,128)(2,1)S(1)}, bf16[1,16,1024]{2,1,0:T(8,128)(2,1)S(1)}, u32[]{:S(2)}, u32[]{:S(2)}) collective-permute-start(bf16[1,16,1024]{2,1,0:T(8,128)(2,1)S(1)} %get-tuple-element.6), channel_id=1, source_target_pairs={{0,1},{1,2},{2,3},{4,5},{5,6},{6,7},{8,9},{9,10},{10,11},{12,13},{... | collective-permute-start | bytes 98312 | tf_op jit(solution)/shard_map/ppermute | solution.py:525
  7.6 0.0 copy-start
  7.7 0.0 copy-start.2
  7.7 0.0 copy-start.4
  7.7 0.0 copy-start.5
  7.7 1.4 %collective-permute-start.2 = (bf16[1,16,1024]{2,1,0:T(8,128)(2,1)S(1)}, bf16[1,16,1024]{2,1,0:T(8,128)(2,1)S(1)}, u32[]{:S(2)}, u32[]{:S(2)}) collective-permute-start(bf16[1,16,1024]{2,1,0:T(8,128)(2,1)S(1)} %get-tuple-element.7), channel_id=1, source_target_pairs={{1,0},{2,1},{3,2},{5,4},{6,5},{7,6},{9,8},{10,9},{11,10},{13,12},{... | collective-permute-start | bytes 98312 | tf_op jit(solution)/shard_map/ppermute | solution.py:526
  9.1 5.9 %patch_spectra.1.own_patch = f32[1,4,8,128,256]{4,3,2,1,0:T(8,128)S(1)} custom-call(bf16[1,1024,1024]{2,1,0:T(8,128)(2,1)} %image_ref.3, bf16[512,256]{1,0:T(8,128)(2,1)} %constant.17.clone.along_ref, bf16[256,256]{1,0:T(8,128)(2,1)} %constant.18.clone.down_ref), custom_call_target="tpu_custom_call" | custom-call | flops 5000000000 | bytes 10000000 | tf_op jit(solution)/shard_map/patch_spectra/pallas_call | solution.py:425
  15.0 0.0 copy-start.8
  15.0 2.0 %copy-done.8 = f32[1,4,8,128,256]{4,3,2,1,0:T(8,128)} copy-done((f32[1,4,8,128,256]{4,3,2,1,0:T(8,128)}, f32[1,4,8,128,256]{4,3,2,1,0:T(8,128)S(1)}, u32[]{:S(2)}) %copy-start.8) | copy-done | bytes 4194328
  17.0 0.0 collective-permute-done.1.low_ref
  17.0 0.0 collective-permute-done.2.high_ref
  17.0 0.0 copy-start.1
  17.0 0.0 copy-start.3
  17.0 0.0 copy-start.6
  17.0 0.0 copy-start.7
  17.0 0.0 copy-start.9
  17.0 1.6 %collective-permute-start.3 = (bf16[1,32,1024]{2,1,0:T(8,128)(2,1)S(1)}, bf16[1,32,1024]{2,1,0:T(8,128)(2,1)S(1)}, u32[]{:S(2)}, u32[]{:S(2)}) collective-permute-start(bf16[1,32,1024]{2,1,0:T(8,128)(2,1)S(1)} %pad_maximum_fusion), channel_id=1, source_target_pairs={{4,0},{8,4},{12,8},{16,12},{20,16},{24,20},{28,24},{5,1},{9,5},{13... | collective-permute-start | bytes 196616 | tf_op jit(solution)/shard_map/ppermute | solution.py:527
  18.6 0.0 copy-done
  18.6 0.0 copy-done.2
  18.6 0.0 copy-done.4
  18.6 0.0 copy-done.5
  18.6 6.3 %window_spectra.1.own_window = f32[1,4,8,128,256]{4,3,2,1,0:T(8,128)S(1)} custom-call(s32[1,2,8,8]{3,2,1,0:T(8,128)S(1)} %copy-done.2, bf16[1,1024,1024]{2,1,0:T(8,128)(2,1)S(1)} %copy-done, bf16[1,16,1024]{2,1,0:T(8,128)(2,1)S(1)} %collective-permute-done.1.low_ref, bf16[1,16,1024]{2,1,0:T(8,128)(2,1)S(1)} %collective-permute-done.2.high_ref, ...), custom_call_target="tpu_custom_call" | custom-call | flops 5000000000 | bytes 10000000 | tf_op jit(solution)/shard_map/window_spectra/pallas_call | solution.py:446
  24.9 0.0 collective-permute-done.3
  25.0 0.0 collective-permute-done.image_ref
  25.0 0.0 copy-done.1
  25.0 0.0 copy-done.3
  25.0 0.0 copy-done.6
  25.0 13.5 %pair_flows.1 = (f32[1,2,8,8]{3,2,1,0:T(8,128)}, f32[32,1,2,128]{3,2,1,0:T(2,128)S(1)}) custom-call(s32[1]{0:T(128)} %bitcast.place_ref, s32[1,2,8,8]{3,2,1,0:T(8,128)S(1)} %copy-done.1, bf16[1,1024,1024]{2,1,0:T(8,128)(2,1)} %collective-permute-done.image_ref, bf16[1,16,1024]{2,1,0:T(8,128)(2,1)S(1)} %get-tuple-element.9.low_ref, ...), custom_call_target="tpu_custom_call" | custom-call | flops 20000000000 | bytes 10000000 | tf_op jit(solution)/shard_map/pair_flows/pallas_call | solution.py:477
  38.5 17.7 %all_to_all.5 = f32[32,1,2,128]{3,2,1,0:T(2,128)S(1)} all-to-all(f32[32,1,2,128]{3,2,1,0:T(2,128)S(1)} %get-tuple-element.5), channel_id=1, replica_groups=mesh['sec'=8,'tile'=4] {'sec','tile'}, dimensions={0} | all-to-all | bytes 65536 | tf_op jit(solution)/shard_map/all_to_all | solution.py:539
  56.2 1.1 %relax.1 = f32[1,2,8,8]{3,2,1,0:T(8,128)} custom-call(f32[32,2,128]{2,1,0:T(2,128)S(1)} %bitcast.2), custom_call_target="tpu_custom_call" | custom-call | tf_op jit(solution)/shard_map/relax/pallas_call | solution.py:545
  (4 shorter events, 0.0 us)
Async XLA Ops:
  0.6 24.3 %collective-permute-start = (bf16[1,1024,1024]{2,1,0:T(8,128)(2,1)}, bf16[1,1024,1024]{2,1,0:T(8,128)(2,1)}, u32[]{:S(2)}, u32[]{:S(2)}) collective-permute-start(bf16[1,1024,1024]{2,1,0:T(8,128)(2,1)} %image_ref.3), channel_id=1, source_target_pairs={{4,0},{8,4},{12,8},{16,12},{20,16},{24,20},{28,24},{5,1},{9,5},{13... | collective-permute-start | bytes 6291464 | tf_op jit(solution)/shard_map/ppermute | solution.py:522
  2.7 14.2 %collective-permute-start.1 = (bf16[1,16,1024]{2,1,0:T(8,128)(2,1)S(1)}, bf16[1,16,1024]{2,1,0:T(8,128)(2,1)S(1)}, u32[]{:S(2)}, u32[]{:S(2)}) collective-permute-start(bf16[1,16,1024]{2,1,0:T(8,128)(2,1)S(1)} %get-tuple-element.6), channel_id=1, source_target_pairs={{0,1},{1,2},{2,3},{4,5},{5,6},{6,7},{8,9},{9,10},{10,11},{12,13},{... | collective-permute-start | bytes 98312 | tf_op jit(solution)/shard_map/ppermute | solution.py:525
  7.6 11.0 %copy-start = (bf16[1,1024,1024]{2,1,0:T(8,128)(2,1)S(1)}, bf16[1,1024,1024]{2,1,0:T(8,128)(2,1)}, u32[]{:S(2)}) copy-start(bf16[1,1024,1024]{2,1,0:T(8,128)(2,1)} %image_ref.3) | copy-start | bytes 6291460
  7.7 11.0 %copy-start.2 = (s32[1,2,8,8]{3,2,1,0:T(8,128)S(1)}, s32[1,2,8,8]{3,2,1,0:T(8,128)}, u32[]{:S(2)}) copy-start(s32[1,2,8,8]{3,2,1,0:T(8,128)} %bwd_ref.1) | copy-start | bytes 1540
  7.7 11.0 %copy-start.4 = (bf16[512,256]{1,0:T(8,128)(2,1)S(1)}, bf16[512,256]{1,0:T(8,128)(2,1)}, u32[]{:S(2)}) copy-start(bf16[512,256]{1,0:T(8,128)(2,1)} %constant.17.clone.along_ref) | copy-start | bytes 786436
  7.7 11.0 %copy-start.5 = (bf16[256,256]{1,0:T(8,128)(2,1)S(1)}, bf16[256,256]{1,0:T(8,128)(2,1)}, u32[]{:S(2)}) copy-start(bf16[256,256]{1,0:T(8,128)(2,1)} %constant.18.clone.down_ref) | copy-start | bytes 393220
  7.7 9.3 %collective-permute-start.2 = (bf16[1,16,1024]{2,1,0:T(8,128)(2,1)S(1)}, bf16[1,16,1024]{2,1,0:T(8,128)(2,1)S(1)}, u32[]{:S(2)}, u32[]{:S(2)}) collective-permute-start(bf16[1,16,1024]{2,1,0:T(8,128)(2,1)S(1)} %get-tuple-element.7), channel_id=1, source_target_pairs={{1,0},{2,1},{3,2},{5,4},{6,5},{7,6},{9,8},{10,9},{11,10},{13,12},{... | collective-permute-start | bytes 98312 | tf_op jit(solution)/shard_map/ppermute | solution.py:526
  15.0 2.0 %copy-start.8 = (f32[1,4,8,128,256]{4,3,2,1,0:T(8,128)}, f32[1,4,8,128,256]{4,3,2,1,0:T(8,128)S(1)}, u32[]{:S(2)}) copy-start(f32[1,4,8,128,256]{4,3,2,1,0:T(8,128)S(1)} %patch_spectra.1.own_patch) | copy-start | bytes 12582916
  17.0 8.0 %copy-start.1 = (s32[1,2,8,8]{3,2,1,0:T(8,128)S(1)}, s32[1,2,8,8]{3,2,1,0:T(8,128)}, u32[]{:S(2)}) copy-start(s32[1,2,8,8]{3,2,1,0:T(8,128)} %fwd_ref.1) | copy-start | bytes 1540
  17.0 8.0 %copy-start.3 = (s32[1,8,8]{2,1,0:T(8,128)S(1)}, s32[1,8,8]{2,1,0:T(8,128)}, u32[]{:S(2)}) copy-start(s32[1,8,8]{2,1,0:T(8,128)} %valid_ref.1) | copy-start | bytes 772
  17.0 8.0 %copy-start.6 = (bf16[256,256]{1,0:T(8,128)(2,1)S(1)}, bf16[256,256]{1,0:T(8,128)(2,1)}, u32[]{:S(2)}) copy-start(bf16[256,256]{1,0:T(8,128)(2,1)} %constant.20.clone.cols_ref) | copy-start | bytes 393220
  17.0 8.0 %copy-start.7 = (bf16[128,256]{1,0:T(8,128)(2,1)S(1)}, bf16[128,256]{1,0:T(8,128)(2,1)}, u32[]{:S(2)}) copy-start(bf16[128,256]{1,0:T(8,128)(2,1)} %constant.19.clone.rows_ref) | copy-start | bytes 196612
  17.0 8.0 %copy-start.9 = (f32[1,4,8,128,256]{4,3,2,1,0:T(8,128)S(1)}, f32[1,4,8,128,256]{4,3,2,1,0:T(8,128)}, u32[]{:S(2)}) copy-start(f32[1,4,8,128,256]{4,3,2,1,0:T(8,128)} %copy-done.8) | copy-start | bytes 12582916
  17.0 7.9 %collective-permute-start.3 = (bf16[1,32,1024]{2,1,0:T(8,128)(2,1)S(1)}, bf16[1,32,1024]{2,1,0:T(8,128)(2,1)S(1)}, u32[]{:S(2)}, u32[]{:S(2)}) collective-permute-start(bf16[1,32,1024]{2,1,0:T(8,128)(2,1)S(1)} %pad_maximum_fusion), channel_id=1, source_target_pairs={{4,0},{8,4},{12,8},{16,12},{20,16},{24,20},{28,24},{5,1},{9,5},{13... | collective-permute-start | bytes 196616 | tf_op jit(solution)/shard_map/ppermute | solution.py:527
